TPU v7x, 512 devices: a whole 4x8x8 slice. The times are simulated.
512 devices in a mesh: seq: 64 (over y, x, core), tp: 8 (over z).
Axes of the slice: x: 4, y: 8, z: 8, core: 2. Of those that a mesh axis runs over, the one named last changes fastest.
Arguments:
- q_nope: bfloat16 [4096, 128, 128], P('seq', 'tp'), may hold values from -6 to 6
- q_rope: bfloat16 [4096, 8192], P('seq', 'tp'), may hold values from -16 to 16
- index_queries: bfloat16 [4096, 8192], P('seq', 'tp'), may hold values from -6 to 6
- index_weights: bfloat16 [4096, 64], P('seq', 'tp'), may hold values from -6 to 6
- owner_offsets: int32 [4096, 2], P('seq'), may hold values from 0 to 62, all different within a row; in each aligned block of 64 rows (0 to 63, 64 to 127, ...) at most 4 rows name the same one
- local_blocks: int32 [4096, 2], P('seq'), may hold values from 0 to 13
- key_absorb_weight: bfloat16 [128, 128, 512], P('tp', 'seq'), may hold values from -0.5 to 0.5
- value_expand_weight: bfloat16 [128, 512, 128], P('tp', 'seq'), may hold values from -0.25 to 0.25
- cached_latents: bfloat16 [114688, 512], P('seq'), may hold values from -6 to 6
- rope_keys: bfloat16 [64, 114688], P(None, 'seq'), may hold values from -16 to 16
- index_keys: bfloat16 [114688, 128], P('seq'), may hold values from -6 to 6
Outputs:
- attended: bfloat16 [4096, 16384], P('seq', 'tp')
- index_scores: float32 [4096, 2048], P('seq', 'tp')
Inputs may be any that keep to these rules, and one draw needn't show every extreme that they name: `owner_offsets`: each token names 2 different offsets; the 64 tokens of one index of seq name one offset at most 4 times, a bound that some block reaches.
All inputs are finite; a program needn't handle non-finite values.
Results may differ from a plain program's by a relative error of at most 0.01.
Values may be sent and summed in bfloat16 or wider, within the bound.
No kernel may reach another device: no remote copies, remote signals or barrier semaphores. Data moves between devices by JAX's collectives and lax.ppermute only.
A program may use at most 64 MiB of HBM per device.

v0:
```python
import jax
import jax.numpy as jnp
from jax import lax
from jax.experimental import pallas as pl
from jax.experimental.pallas import tpu as pltpu
from jax.sharding import Mesh
from jax.sharding import PartitionSpec as P

YS, XS, CS = 8, 4, 2
SHARDS = YS * XS * CS
TOK = 64
PICKS = 2
CAP = 4
SLOTS = SHARDS * CAP
ROWS = 2 * SLOTS
HEADS = 16
DIM = 128
ROPE = 64
LATENT = 512
VALUE = 128
IDX_HEADS = 8
IDX_DIM = 128
BLOCK = 128
BLOCKS = 14
SEEN = BLOCKS * BLOCK
GROUP = 16
CHUNK = 128
PER_CHUNK = CHUNK // GROUP
SORTED = 512
SEND = HEADS * DIM + 128
BACK = HEADS * VALUE // 2 + 128
SOFT_SCALE = 192.0 ** (-0.5)
INDEX_SCALE = (128 * 64) ** (-0.5)
F32 = jnp.float32
BF16 = jnp.bfloat16
LIMIT = 56 * 1024 * 1024


def dot(a, b, ca=1, cb=0):
    return lax.dot_general(a, b, (((ca,), (cb,)), ((), ())), preferred_element_type=F32)


def iota(shape, axis):
    return lax.broadcasted_iota(jnp.int32, shape, axis)


def ones_where(mask):
    return jnp.where(mask, 1.0, 0.0).astype(BF16)


def slots_of(dest):
    lane = iota((TOK, SHARDS), 1)
    named = [dest[:, i : i + 1] == lane for i in range(PICKS)]
    both = ones_where(jnp.logical_or(named[0], named[1]))
    below = ones_where(iota((TOK, TOK), 1) < iota((TOK, TOK), 0))
    earlier = dot(below, both)
    return [
        jnp.sum(jnp.where(n, earlier, 0.0), axis=1, keepdims=True).astype(jnp.int32) for n in named
    ]


def pack_kernel(dest_ref, blocks_ref, nope_ref, rope_ref, idx_ref, weights_ref, out_ref):
    dest = dest_ref[...]
    slot = slots_of(dest)
    row = iota((TOK, ROWS), 1)
    left = [row == dest[:, i : i + 1] * 8 + slot[i] for i in range(PICKS)]
    right = [row == dest[:, i : i + 1] * 8 + 4 + slot[i] for i in range(PICKS)]
    left_all = ones_where(jnp.logical_or(left[0], left[1]))
    right_all = ones_where(jnp.logical_or(right[0], right[1]))
    left_each = jnp.concatenate([ones_where(n) for n in left], axis=0)
    queries = jnp.concatenate([rope_ref[...], idx_ref[...]], axis=1)
    nope = nope_ref[...]
    half = SEND - 128
    both = jnp.concatenate([left_all, right_all], axis=0)
    data = jnp.concatenate([nope, queries], axis=0)
    out_ref[:, :half] = dot(both, data, 0, 0).astype(BF16)
    lane = iota((TOK, 128), 1)
    spread = dot(
        weights_ref[...], ones_where(iota((IDX_HEADS, 128), 0) == iota((IDX_HEADS, 128), 1))
    )
    extra = []
    for i in range(PICKS):
        number = blocks_ref[:, i : i + 1].astype(F32)
        extra.append(
            jnp.where(lane == 8, number, jnp.where(lane == 9, 1.0, spread)).astype(BF16)
        )
    out_ref[:, half:] = dot(left_each, jnp.concatenate(extra, axis=0), 0, 0).astype(BF16)


def pick_rows(offset):
    slot = iota((SLOTS, ROWS), 0)
    return ones_where(iota((SLOTS, ROWS), 1) == (slot // CAP) * 8 + offset + slot % CAP)


def far_index_kernel(sent_ref, keys_ref, out_ref, wide_ref):
    half = SEND - 128
    queries = dot(pick_rows(4), sent_ref[:, HEADS * ROPE : half]).astype(BF16)
    extra = dot(pick_rows(0), sent_ref[:, half:])
    block = extra[:, 8:9].astype(jnp.int32)
    for g in range(IDX_HEADS):
        wide_ref[g] = jnp.broadcast_to(extra[:, g : g + 1], (SLOTS, 128))
    result = jnp.zeros((SLOTS, BLOCK), F32)
    for b in range(0, BLOCKS, 2):
        keys = keys_ref[b * BLOCK : (b + 2) * BLOCK, :]
        sums = [jnp.zeros((SLOTS, BLOCK), F32) for _ in range(2)]
        for g in range(IDX_HEADS):
            dots = dot(queries[:, g * IDX_DIM : (g + 1) * IDX_DIM], keys, 1, 1)
            dots = jnp.maximum(dots, 0.0)
            for e in range(2):
                sums[e] = sums[e] + wide_ref[g] * dots[:, e * BLOCK : (e + 1) * BLOCK]
        for e in range(2):
            result = jnp.where(block == b + e, sums[e], result)
    out_ref[...] = result * INDEX_SCALE


def weight_kernel(all_ref, key_ref, value_ref):
    to, at = iota((256, 256), 0), iota((256, 256), 1)
    part = to - 128
    quarter, seq, row = part // 32, (part % 32) // 2, part % 2
    source = jnp.where(to < 128, (to // 8) * 16 + to % 8, seq * 16 + 8 + quarter * 2 + row)
    order = ones_where(at == source)
    for n in range(4):
        for lanes in range(0, 2048, 512):
            sorted_rows = dot(order, all_ref[n * 256 : (n + 1) * 256, lanes : lanes + 512])
            sorted_rows = sorted_rows.astype(BF16)
            value_ref[n * 128 : (n + 1) * 128, lanes : lanes + 512] = sorted_rows[:128]
            for q in range(4):
                key_ref[
                    n * 32 : (n + 1) * 32, q * 2048 + lanes : q * 2048 + lanes + 512
                ] = sorted_rows[128 + q * 32 : 160 + q * 32]


def far_kernel(
    sent_ref, key_ref, value_ref, lat_ref, rot_ref, out_ref,
    where_ref, ql_ref, qr_ref, lat_out_ref, full_ref,
):
    half = SEND - 128
    extra = dot(pick_rows(0), sent_ref[:, half:])
    lane = iota((SLOTS, 128), 1)
    block = extra[:, 8:9].astype(jnp.int32)
    filled = extra[:, 9:10] > 0.5
    mine = jnp.logical_and(lane == block, filled)
    one = ones_where(mine)
    upto = ones_where(iota((SLOTS, SLOTS), 1) <= iota((SLOTS, SLOTS), 0))
    running = dot(upto, one)
    rank = jnp.sum(jnp.where(mine, running, 0.0), axis=1, keepdims=True) - 1.0
    counts = dot(jnp.ones((8, SLOTS), BF16), one)
    groups = jnp.floor((counts + (GROUP - 1.0)) * (1.0 / GROUP))
    before = ones_where(iota((128, 128), 0) < iota((128, 128), 1))
    first = dot(groups.astype(BF16), before)
    last = (first + groups)[0:1, :]
    start = first[0:1, :]
    position = jnp.sum(jnp.where(mine, start, 0.0), axis=1, keepdims=True) * GROUP + rank
    position = jnp.where(filled, position, -1.0).astype(jnp.int32)
    where_ref[...] = ones_where(position == iota((SLOTS, SORTED), 1))
    total = jnp.max(last).astype(jnp.int32)
    narrow = iota((1, 128), 1)

    slot = iota((ROWS, SLOTS), 1)
    base = (slot // CAP) * 8 + slot % CAP
    to_left = ones_where(iota((ROWS, SLOTS), 0) == base)
    to_right = ones_where(iota((ROWS, SLOTS), 0) == base + 4)

    out_ref[...] = jnp.zeros_like(out_ref)

    def chunk(n, _):
        offset = pl.multiple_of(n * CHUNK, CHUNK)
        here = where_ref[:, pl.ds(offset, CHUNK)]
        left = dot(to_left, here).astype(BF16)
        right = dot(to_right, here).astype(BF16)
        nope = dot(left, sent_ref[:, : HEADS * DIM], 0, 0).astype(BF16)
        rope = dot(right, sent_ref[:, : HEADS * ROPE], 0, 0).astype(BF16)
        for h in range(HEADS):
            ql_ref[h] = dot(
                nope[:, h * DIM : (h + 1) * DIM], key_ref[:, h * LATENT : (h + 1) * LATENT]
            ).astype(BF16)
            qr_ref[h] = rope[:, h * ROPE : (h + 1) * ROPE]
        for j in range(PER_CHUNK):
            number = (n * PER_CHUNK + j).astype(F32)
            done = jnp.logical_and(narrow < BLOCKS, last <= number)
            at = jnp.minimum(jnp.sum(jnp.where(done, 1.0, 0.0)).astype(jnp.int32), BLOCKS - 1)
            begin = pl.multiple_of(at * BLOCK, BLOCK)
            latents = lat_ref[pl.ds(begin, BLOCK), :]
            rotary = rot_ref[:, pl.ds(begin, BLOCK)]
            rows = slice(j * GROUP, (j + 1) * GROUP)
            q = ql_ref[:, rows, :].reshape(HEADS * GROUP, LATENT)
            r = qr_ref[:, rows, :].reshape(HEADS * GROUP, ROPE)
            score = (dot(q, latents, 1, 1) + dot(r, rotary)) * SOFT_SCALE
            top = jnp.max(score, axis=1, keepdims=True)
            expo = jnp.exp(score - top)
            total_of = jnp.sum(expo, axis=1, keepdims=True)
            result = dot(expo.astype(BF16), latents).astype(BF16)
            lat_out_ref[:, rows, :] = result.reshape(HEADS, GROUP, LATENT)
            at_lane = iota((GROUP, 128), 1)
            tops = jnp.zeros((GROUP, 128), F32)
            sums = jnp.zeros((GROUP, 128), F32)
            for h in range(HEADS):
                sel = jnp.logical_and(at_lane % HEADS == h, at_lane < 3 * HEADS)
                part = slice(h * GROUP, (h + 1) * GROUP)
                tops = jnp.where(sel, top[part], tops)
                sums = jnp.where(sel, total_of[part], sums)
            for value, place in ((tops, BACK - 128), (sums, 2 * BACK - 128)):
                hi = value.astype(BF16).astype(F32)
                mid = (value - hi).astype(BF16).astype(F32)
                low = value - hi - mid
                split = jnp.where(at_lane < HEADS, hi, jnp.where(at_lane < 2 * HEADS, mid, low))
                full_ref[rows, place : place + 128] = split.astype(BF16)
        for h in range(HEADS):
            value = dot(lat_out_ref[h], value_ref[:, h * VALUE : (h + 1) * VALUE])
            place = h * VALUE if h < HEADS // 2 else h * VALUE + 128
            full_ref[:, place : place + VALUE] = value.astype(BF16)
        back = dot(left, full_ref[:, :BACK]) + dot(right, full_ref[:, BACK:])
        out_ref[...] = (out_ref[...].astype(F32) + back).astype(BF16)
        return 0

    lax.fori_loop(0, (total + PER_CHUNK - 1) // PER_CHUNK, chunk, 0)


def index_kernel(dest_ref, back_ref, idx_ref, weights_ref, keys_ref, out_ref, wide_ref):
    stacked = jnp.concatenate(
        [idx_ref[:, g * IDX_DIM : (g + 1) * IDX_DIM] for g in range(IDX_HEADS)], axis=0
    )
    weights = weights_ref[...].astype(F32)
    for g in range(IDX_HEADS):
        wide_ref[g] = jnp.broadcast_to(weights[:, g : g + 1], (TOK, 256))
    for b in range(0, BLOCKS, 2):
        keys = keys_ref[b * BLOCK : (b + 2) * BLOCK, :]
        dots = jnp.maximum(dot(stacked, keys, 1, 1), 0.0)
        acc = wide_ref[0] * dots[:TOK]
        for g in range(1, IDX_HEADS):
            acc = acc + wide_ref[g] * dots[g * TOK : (g + 1) * TOK]
        out_ref[:, b * BLOCK : (b + 2) * BLOCK] = acc * INDEX_SCALE
    back = back_ref[...]
    hi = back.astype(BF16)
    mid = (back - hi.astype(F32)).astype(BF16)
    low = (back - hi.astype(F32) - mid.astype(F32)).astype(BF16)
    dest = dest_ref[...]
    slot = slots_of(dest)
    lane = iota((TOK, SLOTS), 1)
    for i in range(PICKS):
        pick = ones_where(lane == dest[:, i : i + 1] * CAP + slot[i])
        far = dot(pick, hi) + dot(pick, mid) + dot(pick, low)
        out_ref[:, SEEN + i * BLOCK : SEEN + (i + 1) * BLOCK] = far


def near_kernel(nope_ref, rope_ref, key_ref, value_ref, lat_ref, rot_ref, out_ref, stat_ref):
    lane = iota((TOK, 128), 1)
    stat = jnp.zeros((TOK, 128), F32)
    step = 4
    for first in range(0, HEADS, step):
        heads = range(first, first + step)
        q = jnp.concatenate(
            [
                dot(
                    nope_ref[:, h * DIM : (h + 1) * DIM],
                    key_ref[:, h * LATENT : (h + 1) * LATENT],
                ).astype(BF16)
                for h in heads
            ],
            axis=0,
        )
        r = jnp.concatenate([rope_ref[:, h * ROPE : (h + 1) * ROPE] for h in heads], axis=0)
        score = (dot(q, lat_ref[...], 1, 1) + dot(r, rot_ref[...])) * SOFT_SCALE
        top = jnp.max(score, axis=1, keepdims=True)
        expo = jnp.exp(score - top)
        total = jnp.sum(expo, axis=1, keepdims=True)
        latent = (dot(expo.astype(BF16), lat_ref[...]) / total).astype(BF16)
        for n, h in enumerate(heads):
            part = slice(n * TOK, (n + 1) * TOK)
            value = dot(latent[part], value_ref[:, h * VALUE : (h + 1) * VALUE])
            out_ref[:, h * VALUE : (h + 1) * VALUE] = value.astype(BF16)
            stat = jnp.where(lane == h, top[part], stat)
            stat = jnp.where(lane == HEADS + h, total[part], stat)
    stat_ref[...] = stat


def combine_kernel(dest_ref, back_ref, near_ref, stat_ref, out_ref):
    dest = dest_ref[...]
    slot = slots_of(dest)
    row = iota((TOK, ROWS), 1)
    picks = [row == dest[:, i : i + 1] * 8 + o + slot[i] for i in range(PICKS) for o in (0, 4)]
    got = dot(jnp.concatenate([ones_where(p) for p in picks], axis=0), back_ref[...])
    far_top, far_sum = [], []
    for i in range(PICKS):
        tail = [got[(2 * i + e) * TOK : (2 * i + e + 1) * TOK, BACK - 128 :] for e in range(2)]
        whole = [
            t[:, :HEADS] + t[:, HEADS : 2 * HEADS] + t[:, 2 * HEADS : 3 * HEADS] for t in tail
        ]
        far_top.append(whole[0])
        far_sum.append(whole[1])
    near_top = stat_ref[:, :HEADS]
    near_sum = stat_ref[:, HEADS : 2 * HEADS]
    top = jnp.maximum(near_top, jnp.maximum(far_top[0], far_top[1]))
    near = jnp.exp(near_top - top) * near_sum
    far = [jnp.exp(far_top[i] - top) * far_sum[i] for i in range(PICKS)]
    whole = near + far[0] + far[1]
    near = near / whole
    far = [f / whole for f in far]
    for h in range(HEADS):
        e, place = (0, h) if h < HEADS // 2 else (1, h - HEADS // 2)
        lanes = slice(place * VALUE, (place + 1) * VALUE)
        value = near[:, h : h + 1] * near_ref[:, h * VALUE : (h + 1) * VALUE].astype(F32)
        for i in range(PICKS):
            part = got[(2 * i + e) * TOK : (2 * i + e + 1) * TOK, lanes]
            value = value + far[i][:, h : h + 1] * part
        out_ref[:, h * VALUE : (h + 1) * VALUE] = value.astype(BF16)


def call(kernel, out, scratch=(), name=None, flops=10**9, moved=10**6):
    return pl.pallas_call(
        kernel,
        out_shape=out,
        scratch_shapes=list(scratch),
        compiler_params=pltpu.CompilerParams(vmem_limit_bytes=LIMIT),
        cost_estimate=pl.CostEstimate(flops=flops, bytes_accessed=moved, transcendentals=0),
        name=name,
    )


def shape(dims, dtype=BF16):
    return jax.ShapeDtypeStruct(dims, dtype)


def pack(dest, blocks, nope, rope, idx, weights):
    return call(pack_kernel, shape((ROWS, SEND)), name="pack")(
        dest, blocks, nope, rope, idx, weights
    )


def far_index(sent, keys):
    return call(
        far_index_kernel,
        shape((SLOTS, BLOCK), F32),
        [pltpu.VMEM((IDX_HEADS, SLOTS, 128), F32)],
        name="far_index",
        flops=4 * 10**9,
    )(sent, keys)


def order_weights(gathered):
    return call(
        weight_kernel,
        [shape((DIM, HEADS * LATENT)), shape((LATENT, HEADS * VALUE))],
        name="order_weights",
        flops=4 * 10**9,
    )(gathered)


def far_attention(sent, key, value, lat, rot):
    return call(
        far_kernel,
        shape((ROWS, BACK)),
        [
            pltpu.VMEM((SLOTS, SORTED), BF16),
            pltpu.VMEM((HEADS, CHUNK, LATENT), BF16),
            pltpu.VMEM((HEADS, CHUNK, ROPE), BF16),
            pltpu.VMEM((HEADS, CHUNK, LATENT), BF16),
            pltpu.VMEM((CHUNK, 2 * BACK), BF16),
        ],
        name="far_attention",
        flops=8 * 10**9,
    )(sent, key, value, lat, rot)


def index_terms(dest, back, idx, weights, keys):
    return call(
        index_kernel,
        shape((TOK, SEEN + PICKS * BLOCK), F32),
        [pltpu.VMEM((IDX_HEADS, TOK, 256), F32)],
        name="index_terms",
    )(dest, back, idx, weights, keys)


def near_attention(nope, rope, key, value, lat, rot):
    return call(
        near_kernel,
        [shape((TOK, HEADS * VALUE)), shape((TOK, 128), F32)],
        name="near_attention",
        flops=8 * 10**9,
    )(nope, rope, key, value, lat, rot)


def combine(dest, back, near, stat):
    return call(combine_kernel, shape((TOK, HEADS * VALUE)), name="combine")(
        dest, back, near, stat
    )


SEQ = ("y", "x", "core")


def exchange(value):
    return lax.all_to_all(value, SEQ, split_axis=0, concat_axis=0, tiled=True)


def on_device(
    q_nope,
    q_rope,
    index_queries,
    index_weights,
    owner_offsets,
    local_blocks,
    key_absorb_weight,
    value_expand_weight,
    cached_latents,
    rope_keys,
    index_keys,
):
    here = lax.axis_index(SEQ)
    key_rows = jnp.transpose(key_absorb_weight.reshape(4, 4, 2, LATENT), (0, 2, 1, 3))
    value_rows = jnp.transpose(value_expand_weight, (1, 0, 2))
    shard = jnp.concatenate(
        [value_rows.reshape(8, HEADS * VALUE), key_rows.reshape(8, 4 * LATENT)], axis=0
    )
    gathered = lax.all_gather(shard, SEQ, axis=0, tiled=True)
    dest = (here + 1 + owner_offsets) % SHARDS
    nope = q_nope.reshape(TOK, HEADS * DIM)
    packed = pack(dest, local_blocks, nope, q_rope, index_queries, index_weights)
    sent = exchange(packed.reshape(SHARDS, 8, SEND)).reshape(ROWS, SEND)
    far_scores = far_index(sent, index_keys)
    far_scores = exchange(far_scores.reshape(SHARDS, CAP, BLOCK)).reshape(SLOTS, BLOCK)
    key, value = order_weights(gathered)
    back = far_attention(sent, key, value, cached_latents, rope_keys)
    back = exchange(back.reshape(SHARDS, 8, BACK)).reshape(ROWS, BACK)
    terms = index_terms(dest, far_scores, index_queries, index_weights, index_keys)
    index_scores = lax.psum_scatter(terms, "tp", scatter_dimension=1, tiled=True)
    near, stat = near_attention(nope, q_rope, key, value, cached_latents, rope_keys)
    attended = combine(dest, back, near, stat)
    return (attended, index_scores)


def solution(mesh):
    split = Mesh(mesh.devices.reshape(YS, XS, CS, mesh.shape["tp"]), ("y", "x", "core", "tp"))
    return jax.shard_map(
        on_device,
        mesh=split,
        in_specs=(
            P(SEQ, "tp", None),
            P(SEQ, "tp"),
            P(SEQ, "tp"),
            P(SEQ, "tp"),
            P(SEQ, None),
            P(SEQ, None),
            P("tp", SEQ, None),
            P("tp", SEQ, None),
            P(SEQ, None),
            P(None, SEQ),
            P(SEQ, None),
        ),
        out_specs=(P(SEQ, "tp"), P(SEQ, "tp")),
        check_vma=False,
    )
```

profile of v0, /device:TPU:2, one launch (start us, length us, event | category | flops | bytes accessed | tf_op | source)
XLA Modules:
  0.0 192.5 jit_solution(2209060134226738683)
XLA Ops:
  8.0 0.0 all-gather.2.cloned.1.call-start
  8.0 0.8 copy.30
  8.8 1.4 pad_maximum_fusion
  10.2 0.0 all-gather.2.cloned.1.call-update
  10.3 0.7 broadcast_compare_fusion
  10.9 0.1 copy.27
  11.1 1.4 copy.29.weights_ref
  12.4 0.1 copy.24
  12.5 1.4 copy.28.blocks_ref
  13.9 1.7 copy.35
  15.6 0.6 add_select_fusion.dest_ref
  16.2 3.9 %pack.1 = bf16[512,2176]{1,0:T(8,128)(2,1)} custom-call(s32[64,2]{1,0:T(8,128)} %add_select_fusion.dest_ref, s32[64,2]{1,0:T(8,128)} %copy.28.blocks_ref, bf16[64,2048]{1,0:T(8,128)(2,1)} %bitcast.24, bf16[64,1024]{1,0:T(8,128)(2,1)} %rope_ref.3, bf16[64,1024]{1,0:T(8,128)(2,1)} %idx_ref.3, bf16[64,8]{1,0:T(8,128)(2,1)} %copy.29.weights_ref), custom_call_target="tpu_custom_call" | custom-call | flops 1000000000 | bytes 1000000 | tf_op jit(solution)/shard_map/pack/pallas_call | solution.py:325
  20.1 70.3 %all_to_all.15 = bf16[64,8,2176]{2,1,0:T(8,128)(2,1)} all-to-all(bf16[64,8,2176]{2,1,0:T(8,128)(2,1)} %bitcast.20), channel_id=1, replica_groups=mesh['y'=8,'x'=4,'core'=2,'tp'=8] {'y','x','core'}, dimensions={0} | all-to-all | bytes 4456448 | tf_op jit(solution)/shard_map/all_to_all | solution.py:393
  90.5 5.0 %far_index.1 = f32[256,128]{1,0:T(8,128)} custom-call(bf16[512,2176]{1,0:T(8,128)(2,1)} %bitcast.18, bf16[1792,128]{1,0:T(8,128)(2,1)} %keys_ref.3), custom_call_target="tpu_custom_call" | custom-call | flops 4000000000 | bytes 1000000 | tf_op jit(solution)/shard_map/far_index/pallas_call | solution.py:331
  95.4 5.6 %all-to-all-start.2 = ((f32[64,4,128]{2,1,0:T(4,128)}), f32[64,4,128]{2,1,0:T(4,128)S(1)}, u32[]{:S(2)}, u32[]{:S(2)}) async-start(f32[64,4,128]{2,1,0:T(4,128)} %bitcast.27), calls=%async_computation.2 | async-start | bytes 262144 | tf_op jit(solution)/shard_map/all_to_all | solution.py:393
  101.1 7.4 %all-gather.2.cloned.1.call-done.all_ref = bf16[1024,2048]{1,0:T(8,128)(2,1)} async-done(((bf16[16,2048]{1,0:T(8,128)(2,1)}), bf16[1024,2048]{1,0:T(8,128)(2,1)}) %all-gather.2.cloned.1.call-update) | async-done | bytes 4194320 | tf_op jit(solution)/shard_map/all_gather | solution.py:415
  108.5 5.5 %order_weights.1 = (bf16[128,8192]{1,0:T(8,128)(2,1)}, bf16[512,2048]{1,0:T(8,128)(2,1)}) custom-call(bf16[1024,2048]{1,0:T(8,128)(2,1)} %all-gather.2.cloned.1.call-done.all_ref), custom_call_target="tpu_custom_call" | custom-call | flops 4000000000 | bytes 1000000 | tf_op jit(solution)/shard_map/order_weights/pallas_call | solution.py:341
  113.9 17.1 %far_attention.1 = bf16[512,1152]{1,0:T(8,128)(2,1)} custom-call(bf16[512,2176]{1,0:T(8,128)(2,1)} %bitcast.19, bf16[128,8192]{1,0:T(8,128)(2,1)} %get-tuple-element.6.key_ref, bf16[512,2048]{1,0:T(8,128)(2,1)} %get-tuple-element.7.value_ref, bf16[1792,512]{1,0:T(8,128)(2,1)} %lat_ref.3, bf16[64,1792]{1,0:T(8,128)(2,1)} %rot_ref.3), custom_call_target="tpu_custom_call" | custom-call | flops 8000000000 | bytes 1000000 | tf_op jit(solution)/shard_map/far_attention/pallas_call | solution.py:350
  131.1 0.0 all-to-all-done.2
  131.1 0.0 copy-start.1
  131.1 9.0 %all-to-all-start.1 = ((bf16[64,8,1152]{2,1,0:T(8,128)(2,1)}), bf16[64,8,1152]{2,1,0:T(8,128)(2,1)S(1)}, u32[]{:S(2)}, u32[]{:S(2)}) async-start(bf16[64,8,1152]{2,1,0:T(8,128)(2,1)} %bitcast.22), calls=%async_computation.1 | async-start | bytes 2359296 | tf_op jit(solution)/shard_map/all_to_all | solution.py:393
  140.1 0.3 reduce-scatter.2.cloned.1.call-start
  140.4 0.0 copy-done.1
  140.4 3.2 %index_terms.1 = f32[64,2048]{1,0:T(8,128)} custom-call(s32[64,2]{1,0:T(8,128)} %add_select_fusion.dest_ref, f32[256,128]{1,0:T(8,128)} %bitcast.26, bf16[64,1024]{1,0:T(8,128)(2,1)} %idx_ref.3, bf16[64,8]{1,0:T(8,128)(2,1)} %copy.29.weights_ref, bf16[1792,128]{1,0:T(8,128)(2,1)} %keys_ref.3), custom_call_target="tpu_custom_call" | custom-call | flops 1000000000 | bytes 1000000 | tf_op jit(solution)/shard_map/index_terms/pallas_call | solution.py:366
  143.6 0.0 reduce-scatter.2.cloned.1.call-update
  143.6 10.9 %near_attention.1 = (bf16[64,2048]{1,0:T(8,128)(2,1)}, f32[64,128]{1,0:T(8,128)}) custom-call(bf16[64,2048]{1,0:T(8,128)(2,1)} %bitcast.25, bf16[64,1024]{1,0:T(8,128)(2,1)} %rope_ref.3, bf16[128,8192]{1,0:T(8,128)(2,1)} %get-tuple-element.6.key_ref, bf16[512,2048]{1,0:T(8,128)(2,1)} %get-tuple-element.7.value_ref, bf16[1792,512]{1,0:T(8,128)(2,1)} %lat_ref.3, ...), custom_call_target="tpu_custom_call" | custom-call | flops 8000000000 | bytes 1000000 | tf_op jit(solution)/shard_map/near_attention/pallas_call | solution.py:375
  154.6 17.1 %all-to-all-done.1 = bf16[64,8,1152]{2,1,0:T(8,128)(2,1)S(1)} async-done(((bf16[64,8,1152]{2,1,0:T(8,128)(2,1)}), bf16[64,8,1152]{2,1,0:T(8,128)(2,1)S(1)}, u32[]{:S(2)}, u32[]{:S(2)}) %all-to-all-start.1) | async-done | bytes 1179680 | tf_op jit(solution)/shard_map/all_to_all | solution.py:393
  171.7 0.0 copy-start
  171.7 1.0 copy-done
  172.7 3.5 %combine.1 = bf16[64,2048]{1,0:T(8,128)(2,1)} custom-call(s32[64,2]{1,0:T(8,128)} %add_select_fusion.dest_ref, bf16[512,1152]{1,0:T(8,128)(2,1)} %bitcast.21, bf16[64,2048]{1,0:T(8,128)(2,1)} %get-tuple-element.8.near_ref, f32[64,128]{1,0:T(8,128)} %get-tuple-element.9.stat_ref), custom_call_target="tpu_custom_call" | custom-call | flops 1000000000 | bytes 1000000 | tf_op jit(solution)/shard_map/combine/pallas_call | solution.py:384
  176.2 8.8 %reduce-scatter.2.cloned.1.call-done = f32[64,256]{1,0:T(8,128)} async-done(((f32[64,2048]{1,0:T(8,128)}), f32[64,256]{1,0:T(8,128)}) %reduce-scatter.2.cloned.1.call-update) | async-done | bytes 65552 | tf_op jit(solution)/shard_map/reduce_scatter | solution.py:426
  (1 shorter events, 0.0 us)
Async XLA Ops:
  8.0 100.5 %all-gather.2.cloned.1.call-start = ((), (), s32[]{:S(2)}) async-start(), calls=%async_computation.4 | async-start | bytes 4259840 | tf_op jit(solution)/shard_map/all_gather | solution.py:415
  95.4 35.6 %all-to-all-start.2 = ((f32[64,4,128]{2,1,0:T(4,128)}), f32[64,4,128]{2,1,0:T(4,128)S(1)}, u32[]{:S(2)}, u32[]{:S(2)}) async-start(f32[64,4,128]{2,1,0:T(4,128)} %bitcast.27), calls=%async_computation.2 | async-start | bytes 262144 | tf_op jit(solution)/shard_map/all_to_all | solution.py:393
  131.1 9.3 %copy-start.1 = (f32[64,4,128]{2,1,0:T(4,128)}, f32[64,4,128]{2,1,0:T(4,128)S(1)}, u32[]{:S(2)}) copy-start(f32[64,4,128]{2,1,0:T(4,128)S(1)} %all-to-all-done.2) | copy-start | bytes 393220
  131.1 40.6 %all-to-all-start.1 = ((bf16[64,8,1152]{2,1,0:T(8,128)(2,1)}), bf16[64,8,1152]{2,1,0:T(8,128)(2,1)S(1)}, u32[]{:S(2)}, u32[]{:S(2)}) async-start(bf16[64,8,1152]{2,1,0:T(8,128)(2,1)} %bitcast.22), calls=%async_computation.1 | async-start | bytes 2359296 | tf_op jit(solution)/shard_map/all_to_all | solution.py:393
  140.1 44.9 %reduce-scatter.2.cloned.1.call-start = ((), (), s32[]{:S(2)}) async-start(), calls=%async_computation.5 | async-start | bytes 589824 | tf_op jit(solution)/shard_map/reduce_scatter | solution.py:426
  171.7 1.0 copy-start
Sparse Core Ops, SparseCore 0:
  12.8 95.6 all-gather.1
Sparse Core Ops, SparseCore 1:
  143.9 41.0 reduce-scatter.1
where the time goes:
time: 193 us; the launch traced here: 192 us
  blocking collectives  70.3 us (36%)
  Pallas kernels  49.1 us (25%)
  waiting for transfers between devices  33.3 us (17%)
  between operations  15.5 us (8%)
  starting transfers between devices  14.9 us (8%)
  local copies, waits for them, and re-layouts  6.49 us (3%)
  other arithmetic  2.7 us (1%)
    all_to_all x1, blocking collectives, exchange(): return lax.all_to_all(value, SEQ, split_axis=0, concat_axis=0, tiled=True)  70.3 us
    pallas_call x1, Pallas kernels, far_attention(): call(far_kernel, shape((ROWS, BACK)), [pltpu.VMEM((SLOTS, SORTED), BF16),...  17.1 us
    all_to_all x2, waiting for transfers between devices, exchange(): return lax.all_to_all(value, SEQ, split_axis=0, concat_axis=0, tiled=True)  17.1 us
    all_to_all x2, starting transfers between devices, exchange(): return lax.all_to_all(value, SEQ, split_axis=0, concat_axis=0, tiled=True)  14.6 us
    pallas_call x1, Pallas kernels, near_attention(): call(near_kernel, [shape((TOK, HEADS * VALUE)), shape((TOK, 128), F32)],...  10.9 us
    reduce_scatter x1, waiting for transfers between devices, on_device(): lax.psum_scatter(terms, 'tp', scatter_dimension=1, tiled=True)  8.79 us
    all_gather x1, waiting for transfers between devices, on_device(): gathered = lax.all_gather(shard, SEQ, axis=0, tiled=True)  7.41 us
    unnamed x8, local copies, waits for them, and re-layouts  5.5 us
  transfers between devices with their start and end apart: 4, of which 3 were waited for; matrix products, arithmetic and copies ran while one was open for 3% of the time, Pallas kernels for 26%

commit v1 on v0

v1 whole, which is shorter than its diff:
```python
import jax
import jax.numpy as jnp
from jax import lax
from jax.experimental import pallas as pl
from jax.experimental.pallas import tpu as pltpu
from jax.sharding import Mesh
from jax.sharding import PartitionSpec as P

YS, XS, CS = 8, 4, 2
SHARDS = YS * XS * CS
TOK = 64
PICKS = 2
CAP = 4
SLOTS = SHARDS * CAP
ROWS = 2 * SLOTS
HEADS = 16
DIM = 128
ROPE = 64
LATENT = 512
VALUE = 128
IDX_HEADS = 8
IDX_DIM = 128
BLOCK = 128
BLOCKS = 14
SEEN = BLOCKS * BLOCK
GROUP = 16
CHUNK = 128
PER_CHUNK = CHUNK // GROUP
SORTED = 512
SEND = HEADS * DIM + 128
BACK = HEADS * VALUE // 2 + 128
SOFT_SCALE = 192.0 ** (-0.5)
INDEX_SCALE = (128 * 64) ** (-0.5)
F32 = jnp.float32
BF16 = jnp.bfloat16


def dot(a, b, ca=1, cb=0):
    return lax.dot_general(a, b, (((ca,), (cb,)), ((), ())), preferred_element_type=F32)


def iota(shape, axis):
    return lax.broadcasted_iota(jnp.int32, shape, axis)


def ones_where(mask):
    return jnp.where(mask, 1.0, 0.0).astype(BF16)


def slots_of(dest):
    lane = iota((TOK, SHARDS), 1)
    named = [dest[:, i : i + 1] == lane for i in range(PICKS)]
    both = ones_where(jnp.logical_or(named[0], named[1]))
    below = ones_where(iota((TOK, TOK), 1) < iota((TOK, TOK), 0))
    earlier = dot(below, both)
    return [
        jnp.sum(jnp.where(n, earlier, 0.0), axis=1, keepdims=True).astype(jnp.int32) for n in named
    ]


def spread_out(value, rows):
    eye = ones_where(iota((rows, 128), 0) == iota((rows, 128), 1))
    return dot(value.astype(BF16), eye, 0, 0)


def pack_kernel(offsets_ref, blocks_ref, weights_ref, nope_ref, rope_ref, idx_ref, out_ref, place_ref):
    here = (lax.axis_index("y") * XS + lax.axis_index("x")) * CS + lax.axis_index("core")
    offsets = spread_out(offsets_ref[...].astype(F32), PICKS).astype(jnp.int32)
    numbers = spread_out(blocks_ref[...].astype(F32), PICKS)
    spread = spread_out(weights_ref[...], IDX_HEADS)
    dest = offsets + (here + 1)
    dest = jnp.where(dest >= SHARDS, dest - SHARDS, dest)
    slot = slots_of(dest)
    row = iota((TOK, ROWS), 1)
    at = [dest[:, i : i + 1] * 8 + slot[i] for i in range(PICKS)]
    left = [row == at[i] for i in range(PICKS)]
    right = [row == at[i] + 4 for i in range(PICKS)]
    lane = iota((TOK, 128), 1)
    place_ref[...] = jnp.where(lane == 0, at[0], at[1])
    left_all = ones_where(jnp.logical_or(left[0], left[1]))
    right_all = ones_where(jnp.logical_or(right[0], right[1]))
    left_each = jnp.concatenate([ones_where(n) for n in left], axis=0)
    queries = jnp.concatenate([rope_ref[...], idx_ref[...]], axis=1)
    half = SEND - 128
    both = jnp.concatenate([left_all, right_all], axis=0)
    data = jnp.concatenate([nope_ref[...], queries], axis=0)
    out_ref[:, :half] = dot(both, data, 0, 0).astype(BF16)
    extra = []
    for i in range(PICKS):
        number = numbers[:, i : i + 1]
        extra.append(
            jnp.where(lane == 8, number, jnp.where(lane == 9, 1.0, spread)).astype(BF16)
        )
    out_ref[:, half:] = dot(left_each, jnp.concatenate(extra, axis=0), 0, 0).astype(BF16)


def pick_rows(offset):
    slot = iota((SLOTS, ROWS), 0)
    return ones_where(iota((SLOTS, ROWS), 1) == (slot // CAP) * 8 + offset + slot % CAP)


def far_index_kernel(sent_ref, keys_ref, out_ref, where_ref, table_ref, wide_ref):
    half = SEND - 128
    queries = dot(pick_rows(4), sent_ref[:, HEADS * ROPE : half]).astype(BF16)
    extra = dot(pick_rows(0), sent_ref[:, half:])
    block = extra[:, 8:9].astype(jnp.int32)
    lane = iota((SLOTS, 128), 1)
    filled = extra[:, 9:10] > 0.5
    mine = jnp.logical_and(lane == block, filled)
    one = ones_where(mine)
    upto = ones_where(iota((SLOTS, SLOTS), 1) <= iota((SLOTS, SLOTS), 0))
    running = dot(upto, one)
    rank = jnp.sum(jnp.where(mine, running, 0.0), axis=1, keepdims=True) - 1.0

    def groups_of(counts):
        return jnp.floor((counts + (GROUP - 1.0)) * (1.0 / GROUP))

    row, column = iota((128, 128), 0), iota((128, 128), 1)
    groups = groups_of(dot(jnp.ones((8, SLOTS), BF16), one))
    first = dot(groups.astype(BF16), ones_where(row < column))[0:1, :]
    position = jnp.sum(jnp.where(mine, first, 0.0), axis=1, keepdims=True) * GROUP + rank
    position = jnp.where(filled, position, -1.0).astype(jnp.int32)
    where_ref[...] = ones_where(position == iota((SLOTS, SORTED), 1))
    down = groups_of(dot(one, jnp.ones((SLOTS, 128), BF16), 0, 0))
    last = dot(ones_where(column <= row), down.astype(BF16))
    done = jnp.logical_and(last <= column.astype(F32), row < BLOCKS)
    block_of = jnp.sum(jnp.where(done, 1.0, 0.0), axis=0, keepdims=True)
    block_of = jnp.minimum(block_of, BLOCKS - 1.0)
    total = jnp.max(last, axis=0, keepdims=True)
    table_ref[...] = jnp.where(iota((8, 128), 0) == 0, block_of, total).astype(jnp.int32)

    for g in range(IDX_HEADS):
        wide_ref[g] = jnp.broadcast_to(extra[:, g : g + 1], (SLOTS, 128))
    result = jnp.zeros((SLOTS, BLOCK), F32)
    for b in range(0, BLOCKS, 2):
        keys = keys_ref[b * BLOCK : (b + 2) * BLOCK, :]
        sums = [jnp.zeros((SLOTS, BLOCK), F32) for _ in range(2)]
        for g in range(IDX_HEADS):
            dots = dot(queries[:, g * IDX_DIM : (g + 1) * IDX_DIM], keys, 1, 1)
            dots = jnp.maximum(dots, 0.0)
            for e in range(2):
                sums[e] = sums[e] + wide_ref[g] * dots[:, e * BLOCK : (e + 1) * BLOCK]
        for e in range(2):
            result = jnp.where(block == b + e, sums[e], result)
    out_ref[...] = result * INDEX_SCALE


def order_weights(all_ref, key_ref, value_ref, ready=None):
    to, at = iota((256, 256), 0), iota((256, 256), 1)
    part = to - 128
    quarter, seq, row = part // 32, (part % 32) // 2, part % 2
    source = jnp.where(to < 128, (to // 8) * 16 + to % 8, seq * 16 + 8 + quarter * 2 + row)
    order = ones_where(at == source)
    for n in range(4):
        if ready is not None:
            ready[n].wait()
        for lanes in range(0, 2048, 512):
            sorted_rows = dot(order, all_ref[n * 256 : (n + 1) * 256, lanes : lanes + 512])
            sorted_rows = sorted_rows.astype(BF16)
            value_ref[n * 128 : (n + 1) * 128, lanes : lanes + 512] = sorted_rows[:128]
            for q in range(4):
                key_ref[
                    n * 32 : (n + 1) * 32, q * 2048 + lanes : q * 2048 + lanes + 512
                ] = sorted_rows[128 + q * 32 : 160 + q * 32]


def far_kernel(
    table_ref, sent_ref, where_ref, index_ref, rot_ref, all_ref, lat_ref, out_ref,
    buffer_ref, held_ref, key_ref, value_ref, ql_ref, qr_ref, lat_out_ref, full_ref, sems,
):
    parts = [
        pltpu.make_async_copy(
            all_ref.at[n * 256 : (n + 1) * 256], buffer_ref.at[n * 256 : (n + 1) * 256], sems.at[n]
        )
        for n in range(4)
    ]
    cache = pltpu.make_async_copy(lat_ref, held_ref, sems.at[4])
    for copy in parts:
        copy.start()
    cache.start()
    slot = iota((ROWS, SLOTS), 1)
    base = (slot // CAP) * 8 + slot % CAP
    to_left = ones_where(iota((ROWS, SLOTS), 0) == base)
    to_right = ones_where(iota((ROWS, SLOTS), 0) == base + 4)
    out_ref[:, : BACK - 128] = jnp.zeros((ROWS, BACK - 128), BF16)
    out_ref[:, BACK - 128 :] = dot(to_right, index_ref[...].astype(BF16)).astype(BF16)
    full_ref[:, 2 * BACK - 128 :] = jnp.zeros((CHUNK, 128), BF16)
    order_weights(buffer_ref, key_ref, value_ref, parts)
    cache.wait()

    def chunk(n, _):
        offset = pl.multiple_of(n * CHUNK, CHUNK)
        here = where_ref[:, pl.ds(offset, CHUNK)]
        left = dot(to_left, here).astype(BF16)
        right = dot(to_right, here).astype(BF16)
        nope = dot(left, sent_ref[:, : HEADS * DIM], 0, 0).astype(BF16)
        rope = dot(right, sent_ref[:, : HEADS * ROPE], 0, 0).astype(BF16)
        for h in range(HEADS):
            ql_ref[h] = dot(
                nope[:, h * DIM : (h + 1) * DIM], key_ref[:, h * LATENT : (h + 1) * LATENT]
            ).astype(BF16)
            qr_ref[h] = rope[:, h * ROPE : (h + 1) * ROPE]
        at_lane = iota((GROUP, 128), 1)
        for j in range(PER_CHUNK):
            begin = pl.multiple_of(table_ref[0, n * PER_CHUNK + j] * BLOCK, BLOCK)
            latents = held_ref[pl.ds(begin, BLOCK), :]
            rotary = rot_ref[:, pl.ds(begin, BLOCK)]
            rows = slice(j * GROUP, (j + 1) * GROUP)
            q = ql_ref[:, rows, :].reshape(HEADS * GROUP, LATENT)
            r = qr_ref[:, rows, :].reshape(HEADS * GROUP, ROPE)
            score = (dot(q, latents, 1, 1) + dot(r, rotary)) * SOFT_SCALE
            top = jnp.max(score, axis=1, keepdims=True)
            expo = jnp.exp(score - top)
            total_of = jnp.sum(expo, axis=1, keepdims=True)
            result = dot(expo.astype(BF16), latents).astype(BF16)
            lat_out_ref[:, rows, :] = result.reshape(HEADS, GROUP, LATENT)
            stat = jnp.zeros((GROUP, 128), F32)
            for h in range(HEADS):
                part = slice(h * GROUP, (h + 1) * GROUP)
                both = jnp.where(at_lane < 3 * HEADS, top[part], total_of[part])
                stat = jnp.where(at_lane % HEADS == h, both, stat)
            hi = stat.astype(BF16).astype(F32)
            mid = (stat - hi).astype(BF16).astype(F32)
            low = stat - hi - mid
            third = (at_lane // HEADS) % 3
            split = jnp.where(third == 0, hi, jnp.where(third == 1, mid, low))
            full_ref[rows, BACK - 128 : BACK] = split.astype(BF16)
        for h in range(HEADS):
            value = dot(lat_out_ref[h], value_ref[:, h * VALUE : (h + 1) * VALUE])
            place = h * VALUE if h < HEADS // 2 else h * VALUE + 128
            full_ref[:, place : place + VALUE] = value.astype(BF16)
        data = jnp.concatenate([full_ref[:, :BACK], full_ref[:, BACK:]], axis=0)
        back = dot(jnp.concatenate([left, right], axis=1), data)
        out_ref[...] = (out_ref[...].astype(F32) + back).astype(BF16)
        return 0

    lax.fori_loop(0, (table_ref[1, 0] + PER_CHUNK - 1) // PER_CHUNK, chunk, 0)


def index_kernel(idx_ref, weights_ref, keys_ref, out_ref, wide_ref):
    stacked = jnp.concatenate(
        [idx_ref[:, g * IDX_DIM : (g + 1) * IDX_DIM] for g in range(IDX_HEADS)], axis=0
    )
    weights = spread_out(weights_ref[...], IDX_HEADS)
    for g in range(IDX_HEADS):
        wide_ref[g] = jnp.broadcast_to(weights[:, g : g + 1], (TOK, 256))
    for b in range(0, BLOCKS, 2):
        keys = keys_ref[b * BLOCK : (b + 2) * BLOCK, :]
        dots = jnp.maximum(dot(stacked, keys, 1, 1), 0.0)
        acc = wide_ref[0] * dots[:TOK]
        for g in range(1, IDX_HEADS):
            acc = acc + wide_ref[g] * dots[g * TOK : (g + 1) * TOK]
        out_ref[b // 2] = acc * INDEX_SCALE
    out_ref[BLOCKS // 2] = jnp.zeros((TOK, 256), F32)


def near_kernel(
    nope_ref, rope_ref, all_ref, lat_ref, rot_ref, out_ref, stat_ref, key_ref, value_ref
):
    order_weights(all_ref, key_ref, value_ref)
    lane = iota((TOK, 128), 1)
    stat = jnp.zeros((TOK, 128), F32)
    step = 4
    for first in range(0, HEADS, step):
        heads = range(first, first + step)
        q = jnp.concatenate(
            [
                dot(
                    nope_ref[:, h * DIM : (h + 1) * DIM],
                    key_ref[:, h * LATENT : (h + 1) * LATENT],
                ).astype(BF16)
                for h in heads
            ],
            axis=0,
        )
        r = jnp.concatenate([rope_ref[:, h * ROPE : (h + 1) * ROPE] for h in heads], axis=0)
        score = (dot(q, lat_ref[...], 1, 1) + dot(r, rot_ref[...])) * SOFT_SCALE
        top = jnp.max(score, axis=1, keepdims=True)
        expo = jnp.exp(score - top)
        total = jnp.sum(expo, axis=1, keepdims=True)
        latent = (dot(expo.astype(BF16), lat_ref[...]) / total).astype(BF16)
        for n, h in enumerate(heads):
            part = slice(n * TOK, (n + 1) * TOK)
            value = dot(latent[part], value_ref[:, h * VALUE : (h + 1) * VALUE])
            out_ref[:, h * VALUE : (h + 1) * VALUE] = value.astype(BF16)
            stat = jnp.where(lane == h, top[part], stat)
            stat = jnp.where(lane == HEADS + h, total[part], stat)
    stat_ref[...] = stat


def combine_kernel(place_ref, back_ref, near_ref, stat_ref, own_ref, out_ref, index_ref):
    row = iota((TOK, ROWS), 1)
    picks = [row == place_ref[:, i : i + 1] + o for i in range(PICKS) for o in (0, 4)]
    got = dot(jnp.concatenate([ones_where(p) for p in picks], axis=0), back_ref[...])
    far_top, far_sum = [], []
    for i in range(PICKS):
        tail = got[2 * i * TOK : (2 * i + 1) * TOK, BACK - 128 :]
        whole = [tail[:, n * HEADS : (n + 1) * HEADS] for n in range(6)]
        far_top.append(whole[0] + whole[1] + whole[2])
        far_sum.append(whole[3] + whole[4] + whole[5])
        terms = got[(2 * i + 1) * TOK : (2 * i + 2) * TOK, BACK - 128 :]
        lanes = slice(i * BLOCK, (i + 1) * BLOCK)
        index_ref[:, lanes] = jnp.where(
            lax.axis_index("tp") == BLOCKS // 2, terms, own_ref[:, lanes]
        )
    near_top = stat_ref[:, :HEADS]
    near_sum = stat_ref[:, HEADS : 2 * HEADS]
    top = jnp.maximum(near_top, jnp.maximum(far_top[0], far_top[1]))
    near = jnp.exp(near_top - top) * near_sum
    far = [jnp.exp(far_top[i] - top) * far_sum[i] for i in range(PICKS)]
    whole = near + far[0] + far[1]
    near = near / whole
    far = [f / whole for f in far]
    for h in range(HEADS):
        e, place = (0, h) if h < HEADS // 2 else (1, h - HEADS // 2)
        lanes = slice(place * VALUE, (place + 1) * VALUE)
        value = near[:, h : h + 1] * near_ref[:, h * VALUE : (h + 1) * VALUE].astype(F32)
        for i in range(PICKS):
            part = got[(2 * i + e) * TOK : (2 * i + e + 1) * TOK, lanes]
            value = value + far[i][:, h : h + 1] * part
        out_ref[:, h * VALUE : (h + 1) * VALUE] = value.astype(BF16)


VMEM = pl.BlockSpec(memory_space=pltpu.VMEM)
SMEM = pl.BlockSpec(memory_space=pltpu.SMEM)


def call(kernel, out, scratch=(), name=None, flops=10**9, limit=16, **more):
    return pl.pallas_call(
        kernel,
        out_shape=out,
        scratch_shapes=list(scratch),
        compiler_params=pltpu.CompilerParams(vmem_limit_bytes=limit * 1024 * 1024),
        cost_estimate=pl.CostEstimate(flops=flops, bytes_accessed=10**6, transcendentals=0),
        name=name,
        **more,
    )


def shape(dims, dtype=BF16):
    return jax.ShapeDtypeStruct(dims, dtype)


def pack(offsets, blocks, weights, nope, rope, idx):
    out = [shape((ROWS, SEND)), shape((TOK, 128), jnp.int32)]
    return call(pack_kernel, out, name="pack")(offsets, blocks, weights, nope, rope, idx)


def far_index(sent, keys):
    out = [
        shape((SLOTS, BLOCK), F32),
        shape((SLOTS, SORTED)),
        shape((8, 128), jnp.int32),
    ]
    scratch = [pltpu.VMEM((IDX_HEADS, SLOTS, 128), F32)]
    return call(far_index_kernel, out, scratch, "far_index", 4 * 10**9)(sent, keys)


WEIGHTS = [
    pltpu.VMEM((DIM, HEADS * LATENT), BF16),
    pltpu.VMEM((LATENT, HEADS * VALUE), BF16),
]


def far_attention(table, sent, where, index, gathered, lat, rot):
    scratch = (
        [pltpu.VMEM((16 * SHARDS, 2048), BF16), pltpu.VMEM((SEEN, LATENT), BF16)]
        + WEIGHTS
        + [
            pltpu.VMEM((HEADS, CHUNK, LATENT), BF16),
            pltpu.VMEM((HEADS, CHUNK, ROPE), BF16),
            pltpu.VMEM((HEADS, CHUNK, LATENT), BF16),
            pltpu.VMEM((CHUNK, 2 * BACK), BF16),
            pltpu.SemaphoreType.DMA((5,)),
        ]
    )
    anywhere = pl.BlockSpec(memory_space=pl.ANY)
    return call(
        far_kernel,
        shape((ROWS, BACK)),
        scratch,
        "far_attention",
        8 * 10**9,
        32,
        in_specs=[SMEM] + [VMEM] * 4 + [anywhere] * 2,
    )(table, sent, where, index, rot, gathered, lat)


def index_terms(idx, weights, keys):
    scratch = [pltpu.VMEM((IDX_HEADS, TOK, 256), F32)]
    return call(index_kernel, shape((8, TOK, 256), F32), scratch, "index_terms")(
        idx, weights, keys
    )


def near_attention(nope, rope, gathered, lat, rot):
    out = [shape((TOK, HEADS * VALUE)), shape((TOK, 128), F32)]
    return call(near_kernel, out, WEIGHTS, "near_attention", 8 * 10**9, 32)(
        nope, rope, gathered, lat, rot
    )


def combine(place, back, near, stat, own):
    out = [shape((TOK, HEADS * VALUE)), shape((TOK, 256), F32)]
    return call(combine_kernel, out, name="combine")(place, back, near, stat, own)


SEQ = ("y", "x", "core")


def exchange(value):
    return lax.all_to_all(value, SEQ, split_axis=0, concat_axis=0, tiled=True)


def on_device(
    q_nope,
    q_rope,
    index_queries,
    index_weights,
    owner_offsets,
    local_blocks,
    key_absorb_weight,
    value_expand_weight,
    cached_latents,
    rope_keys,
    index_keys,
):
    key_rows = jnp.transpose(key_absorb_weight.reshape(4, 4, 2, LATENT), (0, 2, 1, 3))
    value_rows = jnp.transpose(value_expand_weight, (1, 0, 2))
    shard = jnp.concatenate(
        [value_rows.reshape(8, HEADS * VALUE), key_rows.reshape(8, 4 * LATENT)], axis=0
    )
    gathered = lax.all_gather(shard, SEQ, axis=0, tiled=True)
    weights = index_weights.T
    nope = q_nope.reshape(TOK, HEADS * DIM)
    packed, place = pack(owner_offsets.T, local_blocks.T, weights, nope, q_rope, index_queries)
    sent = exchange(packed.reshape(SHARDS, 8, SEND)).reshape(ROWS, SEND)
    terms = index_terms(index_queries, weights, index_keys)
    own = lax.psum_scatter(terms, "tp", scatter_dimension=0, tiled=False)
    index, where, table = far_index(sent, index_keys)
    for bit in (1, 2, 4):
        index = index + lax.ppermute(index, "tp", [(n, n ^ bit) for n in range(8)])
    back = far_attention(table, sent, where, index, gathered, cached_latents, rope_keys)
    back = exchange(back.reshape(SHARDS, 8, BACK)).reshape(ROWS, BACK)
    near, stat = near_attention(nope, q_rope, gathered, cached_latents, rope_keys)
    return combine(place, back, near, stat, own)


def solution(mesh):
    split = Mesh(mesh.devices.reshape(YS, XS, CS, mesh.shape["tp"]), ("y", "x", "core", "tp"))
    return jax.shard_map(
        on_device,
        mesh=split,
        in_specs=(
            P(SEQ, "tp", None),
            P(SEQ, "tp"),
            P(SEQ, "tp"),
            P(SEQ, "tp"),
            P(SEQ, None),
            P(SEQ, None),
            P("tp", SEQ, None),
            P("tp", SEQ, None),
            P(SEQ, None),
            P(None, SEQ),
            P(SEQ, None),
        ),
        out_specs=(P(SEQ, "tp"), P(SEQ, "tp")),
        check_vma=False,
    )
```

time: 193 us -> 205 us (1.062)
  the two profiles are of different devices: /device:TPU:2 before, /device:TPU:4 now
where the time goes in v1:
time: 205 us
  blocking collectives  67.9 us (33%)
  waiting for transfers between devices  44.9 us (22%)
  Pallas kernels  31.9 us (16%)
  starting transfers between devices  28 us (14%)
  between operations  15.7 us (8%)
  local copies, waits for them, and re-layouts  14.8 us (7%)
    all_to_all x1, blocking collectives, exchange(): return lax.all_to_all(value, SEQ, split_axis=0, concat_axis=0, tiled=True)  67.9 us
    reduce_scatter x1, waiting for transfers between devices, on_device(): own = lax.psum_scatter(terms, 'tp', scatter_dimension=0, tiled=False)  30.6 us
    ppermute x3, starting transfers between devices, on_device(): index = index + lax.ppermute(index, 'tp', [(n, n ^ bit) for n in range(8)])  20.5 us
    pallas_call x1, Pallas kernels, far_attention(): call(far_kernel, shape((ROWS, BACK)), scratch, 'far_attention', 8 * 10 **...  15.5 us
    ppermute x3, waiting for transfers between devices, on_device(): index = index + lax.ppermute(index, 'tp', [(n, n ^ bit) for n in range(8)])  14.2 us
    unnamed x36, local copies, waits for them, and re-layouts  14.1 us
    pallas_call x1, Pallas kernels, near_attention(): call(near_kernel, out, WEIGHTS, 'near_attention', 8 * 10 ** 9, 32)  8.49 us
    all_to_all x1, starting transfers between devices, exchange(): return lax.all_to_all(value, SEQ, split_axis=0, concat_axis=0, tiled=True)  7.19 us
  transfers between devices with their start and end apart: 6, of which 4 were waited for; matrix products, arithmetic and copies ran while one was open for 1% of the time, Pallas kernels for 7%

profile of v1, /device:TPU:4, one launch (start us, length us, event | category | flops | bytes accessed | tf_op | source)
XLA Modules:
  0.0 204.6 jit_solution(5649114770359550362)
XLA Ops:
  8.0 0.0 all-gather.2.cloned.1.call-start
  8.0 0.8 copy.13
  8.8 1.4 pad_maximum_fusion
  10.3 1.0 copy.17
  11.3 0.9 copy-done.6
  12.2 0.9 copy-done.8
  13.1 0.7 copy-done.11
  13.8 0.7 copy-done.13
  14.5 0.7 copy-done.14
  15.1 1.4 pack.1
  16.5 67.9 %all_to_all.10 = bf16[64,8,2176]{2,1,0:T(8,128)(2,1)S(1)} all-to-all(bf16[64,8,2176]{2,1,0:T(8,128)(2,1)S(1)} %bitcast.22), channel_id=1, replica_groups=mesh['y'=8,'x'=4,'core'=2,'tp'=8] {'y','x','core'}, dimensions={0} | all-to-all | bytes 4456448 | tf_op jit(solution)/shard_map/all_to_all | solution.py:412
  84.4 3.1 %far_index.1 = (f32[256,128]{1,0:T(8,128)S(1)}, bf16[256,512]{1,0:T(8,128)(2,1)S(1)}, s32[8,128]{1,0:T(8,128)S(1)}) custom-call(bf16[512,2176]{1,0:T(8,128)(2,1)S(1)} %bitcast.20, bf16[1792,128]{1,0:T(8,128)(2,1)S(1)} %copy-done.4), custom_call_target="tpu_custom_call" | custom-call | flops 4000000000 | bytes 1000000 | tf_op jit(solution)/shard_map/far_index/pallas_call | solution.py:356
  87.5 4.6 %collective-permute-start = (f32[256,128]{1,0:T(8,128)S(1)}, f32[256,128]{1,0:T(8,128)S(1)}, u32[]{:S(2)}, u32[]{:S(2)}) collective-permute-start(f32[256,128]{1,0:T(8,128)S(1)} %get-tuple-element.13), channel_id=1, source_target_pairs={{0,1},{1,0},{2,3},{3,2},{4,5},{5,4},{6,7},{7,6},{8,9},{9,8},{10,11... | collective-permute-start | bytes 393224 | tf_op jit(solution)/shard_map/ppermute | solution.py:442
  92.2 3.8 %collective-permute-done = f32[256,128]{1,0:T(8,128)S(1)} collective-permute-done((f32[256,128]{1,0:T(8,128)S(1)}, f32[256,128]{1,0:T(8,128)S(1)}, u32[]{:S(2)}, u32[]{:S(2)}) %collective-permute-start) | collective-permute-done | bytes 131104 | tf_op jit(solution)/shard_map/ppermute | solution.py:442
  96.0 6.7 %collective-permute-start.1 = (f32[256,128]{1,0:T(8,128)S(1)}, f32[256,128]{1,0:T(8,128)S(1)}, u32[]{:S(2)}, u32[]{:S(2)}) collective-permute-start(f32[256,128]{1,0:T(8,128)S(1)} %add.11), channel_id=1, source_target_pairs={{0,2},{1,3},{2,0},{3,1},{4,6},{5,7},{6,4},{7,5},{8,10},{9,11},{10,... | collective-permute-start | bytes 393224 | tf_op jit(solution)/shard_map/ppermute | solution.py:442
  102.7 6.2 %collective-permute-done.1 = f32[256,128]{1,0:T(8,128)S(1)} collective-permute-done((f32[256,128]{1,0:T(8,128)S(1)}, f32[256,128]{1,0:T(8,128)S(1)}, u32[]{:S(2)}, u32[]{:S(2)}) %collective-permute-start.1) | collective-permute-done | bytes 131104 | tf_op jit(solution)/shard_map/ppermute | solution.py:442
  108.9 9.1 %collective-permute-start.2 = (f32[256,128]{1,0:T(8,128)S(1)}, f32[256,128]{1,0:T(8,128)S(1)}, u32[]{:S(2)}, u32[]{:S(2)}) collective-permute-start(f32[256,128]{1,0:T(8,128)S(1)} %add.12), channel_id=1, source_target_pairs={{0,4},{1,5},{2,6},{3,7},{4,0},{5,1},{6,2},{7,3},{8,12},{9,13},{10,... | collective-permute-start | bytes 393224 | tf_op jit(solution)/shard_map/ppermute | solution.py:442
  118.0 4.3 %collective-permute-done.2 = f32[256,128]{1,0:T(8,128)S(1)} collective-permute-done((f32[256,128]{1,0:T(8,128)S(1)}, f32[256,128]{1,0:T(8,128)S(1)}, u32[]{:S(2)}, u32[]{:S(2)}) %collective-permute-start.2) | collective-permute-done | bytes 131104 | tf_op jit(solution)/shard_map/ppermute | solution.py:442
  122.3 0.0 all-gather.2.cloned.1.call-done.all_ref
  122.4 2.2 %copy-done = bf16[1024,2048]{1,0:T(8,128)(2,1)S(1)} copy-done((bf16[1024,2048]{1,0:T(8,128)(2,1)S(1)}, bf16[1024,2048]{1,0:T(8,128)(2,1)}, u32[]{:S(2)}) %copy-start) | copy-done | bytes 4194328
  124.6 1.5 copy-done.2
  126.1 0.9 copy-done.16
  127.0 15.5 %far_attention.1 = bf16[512,1152]{1,0:T(8,128)(2,1)} custom-call(s32[8,128]{1,0:T(8,128)S(1)} %get-tuple-element.11.table_ref, bf16[512,2176]{1,0:T(8,128)(2,1)S(1)} %bitcast.21, bf16[256,512]{1,0:T(8,128)(2,1)S(1)} %copy-done.16, f32[256,128]{1,0:T(8,128)S(1)} %add.13.index_ref, bf16[64,1792]{1,0:T(8,128)(2,1)S(1)} %copy-done.5, ...), custom_call_target="tpu_custom_call" | custom-call | flops 8000000000 | bytes 1000000 | tf_op jit(solution)/shard_map/far_attention/pallas_call | solution.py:378
  142.5 7.2 %all-to-all-start.1 = ((bf16[64,8,1152]{2,1,0:T(8,128)(2,1)}), bf16[64,8,1152]{2,1,0:T(8,128)(2,1)S(1)}, u32[]{:S(2)}, u32[]{:S(2)}) async-start(bf16[64,8,1152]{2,1,0:T(8,128)(2,1)} %bitcast.9), calls=%async_computation.1 | async-start | bytes 2359296 | tf_op jit(solution)/shard_map/all_to_all | solution.py:412
  149.8 0.3 reduce-scatter.2.cloned.1.call-start
  150.0 1.5 index_terms.1
  151.6 2.2 %copy-done.1 = bf16[1024,2048]{1,0:T(8,128)(2,1)S(1)} copy-done((bf16[1024,2048]{1,0:T(8,128)(2,1)S(1)}, bf16[1024,2048]{1,0:T(8,128)(2,1)}, u32[]{:S(2)}) %copy-start.1) | copy-done | bytes 4194328
  153.8 1.5 copy-done.3
  155.3 8.5 %near_attention.1 = (bf16[64,2048]{1,0:T(8,128)(2,1)S(1)}, f32[64,128]{1,0:T(8,128)S(1)}) custom-call(bf16[64,2048]{1,0:T(8,128)(2,1)S(1)} %bitcast.25, bf16[64,1024]{1,0:T(8,128)(2,1)S(1)} %copy-done.9, bf16[1024,2048]{1,0:T(8,128)(2,1)S(1)} %copy-done.1, bf16[1792,512]{1,0:T(8,128)(2,1)S(1)} %copy-done.3, bf16[64,1792]{1,0:T(8,128)(2,1)S(1)} %copy-done.5), custom_call_target="tpu_custom_call" | custom-call | flops 8000000000 | bytes 1000000 | tf_op jit(solution)/shard_map/near_attention/pallas_call | solution.py:398
  163.8 30.6 %reduce-scatter.2.cloned.1.call-done = f32[1,64,256]{2,1,0:T(8,128)} async-done(((f32[8,64,256]{2,1,0:T(8,128)}), f32[1,64,256]{2,1,0:T(8,128)}) %reduce-scatter.2.cloned.1.call-update) | async-done | bytes 65552 | tf_op jit(solution)/shard_map/reduce_scatter | solution.py:439
  194.4 0.8 copy-done.10
  195.3 1.9 combine.1
  (30 shorter events, 0.2 us)
Async XLA Ops:
  8.0 114.4 %all-gather.2.cloned.1.call-start = ((), (), s32[]{:S(2)}) async-start(), calls=%async_computation.3 | async-start | bytes 4259840 | tf_op jit(solution)/shard_map/all_gather | solution.py:433
  11.3 0.9 copy-start.6
  12.2 0.9 copy-start.8
  13.1 0.7 copy-start.11
  13.8 0.7 copy-start.13
  14.5 0.7 copy-start.14
  16.5 67.9 %copy-start.4 = (bf16[1792,128]{1,0:T(8,128)(2,1)S(1)}, bf16[1792,128]{1,0:T(8,128)(2,1)}, u32[]{:S(2)}) copy-start(bf16[1792,128]{1,0:T(8,128)(2,1)} %keys_ref.3) | copy-start | bytes 1376260
  84.4 38.0 %copy-start.5 = (bf16[64,1792]{1,0:T(8,128)(2,1)S(1)}, bf16[64,1792]{1,0:T(8,128)(2,1)}, u32[]{:S(2)}) copy-start(bf16[64,1792]{1,0:T(8,128)(2,1)} %rot_ref.3) | copy-start | bytes 688132
  87.5 30.5 %copy-start.15 = (bf16[256,512]{1,0:T(8,128)(2,1)}, bf16[256,512]{1,0:T(8,128)(2,1)S(1)}, u32[]{:S(2)}) copy-start(bf16[256,512]{1,0:T(8,128)(2,1)S(1)} %get-tuple-element.12.where_ref) | copy-start | bytes 786436
  87.5 8.4 %collective-permute-start = (f32[256,128]{1,0:T(8,128)S(1)}, f32[256,128]{1,0:T(8,128)S(1)}, u32[]{:S(2)}, u32[]{:S(2)}) collective-permute-start(f32[256,128]{1,0:T(8,128)S(1)} %get-tuple-element.13), channel_id=1, source_target_pairs={{0,1},{1,0},{2,3},{3,2},{4,5},{5,4},{6,7},{7,6},{8,9},{9,8},{10,11... | collective-permute-start | bytes 393224 | tf_op jit(solution)/shard_map/ppermute | solution.py:442
  96.0 12.9 %collective-permute-start.1 = (f32[256,128]{1,0:T(8,128)S(1)}, f32[256,128]{1,0:T(8,128)S(1)}, u32[]{:S(2)}, u32[]{:S(2)}) collective-permute-start(f32[256,128]{1,0:T(8,128)S(1)} %add.11), channel_id=1, source_target_pairs={{0,2},{1,3},{2,0},{3,1},{4,6},{5,7},{6,4},{7,5},{8,10},{9,11},{10,... | collective-permute-start | bytes 393224 | tf_op jit(solution)/shard_map/ppermute | solution.py:442
  108.9 13.4 %collective-permute-start.2 = (f32[256,128]{1,0:T(8,128)S(1)}, f32[256,128]{1,0:T(8,128)S(1)}, u32[]{:S(2)}, u32[]{:S(2)}) collective-permute-start(f32[256,128]{1,0:T(8,128)S(1)} %add.12), channel_id=1, source_target_pairs={{0,4},{1,5},{2,6},{3,7},{4,0},{5,1},{6,2},{7,3},{8,12},{9,13},{10,... | collective-permute-start | bytes 393224 | tf_op jit(solution)/shard_map/ppermute | solution.py:442
  122.4 2.2 %copy-start = (bf16[1024,2048]{1,0:T(8,128)(2,1)S(1)}, bf16[1024,2048]{1,0:T(8,128)(2,1)}, u32[]{:S(2)}) copy-start(bf16[1024,2048]{1,0:T(8,128)(2,1)} %all-gather.2.cloned.1.call-done.all_ref) | copy-start | bytes 12582916
  124.6 1.5 copy-start.2
  126.1 0.9 copy-start.16
  142.5 7.5 %copy-start.7 = (bf16[64,1024]{1,0:T(8,128)(2,1)S(1)}, bf16[64,1024]{1,0:T(8,128)(2,1)}, u32[]{:S(2)}) copy-start(bf16[64,1024]{1,0:T(8,128)(2,1)} %idx_ref.3) | copy-start | bytes 393220
  142.5 7.5 %copy-start.12 = (bf16[64,8]{0,1:T(8,128)(2,1)S(1)}, bf16[64,8]{0,1:T(8,128)(2,1)}, u32[]{:S(2)}) copy-start(bf16[64,8]{0,1:T(8,128)(2,1)} %param.14) | copy-start | bytes 3076
  142.5 51.9 %all-to-all-start.1 = ((bf16[64,8,1152]{2,1,0:T(8,128)(2,1)}), bf16[64,8,1152]{2,1,0:T(8,128)(2,1)S(1)}, u32[]{:S(2)}, u32[]{:S(2)}) async-start(bf16[64,8,1152]{2,1,0:T(8,128)(2,1)} %bitcast.9), calls=%async_computation.1 | async-start | bytes 2359296 | tf_op jit(solution)/shard_map/all_to_all | solution.py:412
  149.7 1.8 copy-start.9
  149.8 44.7 %reduce-scatter.2.cloned.1.call-start = ((), (), s32[]{:S(2)}) async-start(), calls=%async_computation.4 | async-start | bytes 589824 | tf_op jit(solution)/shard_map/reduce_scatter | solution.py:439
  151.6 2.2 %copy-start.1 = (bf16[1024,2048]{1,0:T(8,128)(2,1)S(1)}, bf16[1024,2048]{1,0:T(8,128)(2,1)}, u32[]{:S(2)}) copy-start(bf16[1024,2048]{1,0:T(8,128)(2,1)} %all-gather.2.cloned.1.call-done.all_ref) | copy-start | bytes 12582916
  153.8 1.5 copy-start.3
  194.4 0.8 copy-start.10
Sparse Core Ops, SparseCore 0:
  12.8 92.4 all-gather.1
Sparse Core Ops, SparseCore 1:
  153.0 41.3 reduce-scatter.1

commit v2 on v1

--- a/solution.py
+++ b/solution.py
@@ -24,7 +24,8 @@
 BLOCKS = 14
 SEEN = BLOCKS * BLOCK
 GROUP = 16
-CHUNK = 128
+CHUNK = 256
+BATCH = 4
 PER_CHUNK = CHUNK // GROUP
 SORTED = 512
 SEND = HEADS * DIM + 128
@@ -165,7 +166,7 @@
 
 
 def far_kernel(
-    table_ref, sent_ref, where_ref, index_ref, rot_ref, all_ref, lat_ref, out_ref,
+    table_ref, sent_ref, where_ref, rot_ref, all_ref, lat_ref, out_ref,
     buffer_ref, held_ref, key_ref, value_ref, ql_ref, qr_ref, lat_out_ref, full_ref, sems,
 ):
     parts = [
@@ -182,8 +183,7 @@
     base = (slot // CAP) * 8 + slot % CAP
     to_left = ones_where(iota((ROWS, SLOTS), 0) == base)
     to_right = ones_where(iota((ROWS, SLOTS), 0) == base + 4)
-    out_ref[:, : BACK - 128] = jnp.zeros((ROWS, BACK - 128), BF16)
-    out_ref[:, BACK - 128 :] = dot(to_right, index_ref[...].astype(BF16)).astype(BF16)
+    out_ref[...] = jnp.zeros_like(out_ref)
     full_ref[:, 2 * BACK - 128 :] = jnp.zeros((CHUNK, 128), BF16)
     order_weights(buffer_ref, key_ref, value_ref, parts)
     cache.wait()
@@ -201,30 +201,37 @@
             ).astype(BF16)
             qr_ref[h] = rope[:, h * ROPE : (h + 1) * ROPE]
         at_lane = iota((GROUP, 128), 1)
-        for j in range(PER_CHUNK):
-            begin = pl.multiple_of(table_ref[0, n * PER_CHUNK + j] * BLOCK, BLOCK)
-            latents = held_ref[pl.ds(begin, BLOCK), :]
-            rotary = rot_ref[:, pl.ds(begin, BLOCK)]
-            rows = slice(j * GROUP, (j + 1) * GROUP)
-            q = ql_ref[:, rows, :].reshape(HEADS * GROUP, LATENT)
-            r = qr_ref[:, rows, :].reshape(HEADS * GROUP, ROPE)
-            score = (dot(q, latents, 1, 1) + dot(r, rotary)) * SOFT_SCALE
-            top = jnp.max(score, axis=1, keepdims=True)
-            expo = jnp.exp(score - top)
-            total_of = jnp.sum(expo, axis=1, keepdims=True)
-            result = dot(expo.astype(BF16), latents).astype(BF16)
-            lat_out_ref[:, rows, :] = result.reshape(HEADS, GROUP, LATENT)
-            stat = jnp.zeros((GROUP, 128), F32)
-            for h in range(HEADS):
-                part = slice(h * GROUP, (h + 1) * GROUP)
-                both = jnp.where(at_lane < 3 * HEADS, top[part], total_of[part])
-                stat = jnp.where(at_lane % HEADS == h, both, stat)
-            hi = stat.astype(BF16).astype(F32)
-            mid = (stat - hi).astype(BF16).astype(F32)
-            low = stat - hi - mid
-            third = (at_lane // HEADS) % 3
-            split = jnp.where(third == 0, hi, jnp.where(third == 1, mid, low))
-            full_ref[rows, BACK - 128 : BACK] = split.astype(BF16)
+        for first in range(0, PER_CHUNK, BATCH):
+            members = range(first, first + BATCH)
+            caches, scores = [], []
+            for j in members:
+                begin = pl.multiple_of(table_ref[0, n * PER_CHUNK + j] * BLOCK, BLOCK)
+                latents = held_ref[pl.ds(begin, BLOCK), :]
+                rotary = rot_ref[:, pl.ds(begin, BLOCK)]
+                rows = slice(j * GROUP, (j + 1) * GROUP)
+                q = ql_ref[:, rows, :].reshape(HEADS * GROUP, LATENT)
+                r = qr_ref[:, rows, :].reshape(HEADS * GROUP, ROPE)
+                caches.append(latents)
+                scores.append((dot(q, latents, 1, 1) + dot(r, rotary)) * SOFT_SCALE)
+            tops = [jnp.max(score, axis=1, keepdims=True) for score in scores]
+            expos = [jnp.exp(score - top) for score, top in zip(scores, tops)]
+            totals = [jnp.sum(expo, axis=1, keepdims=True) for expo in expos]
+            for j, latents, expo in zip(members, caches, expos):
+                result = dot(expo.astype(BF16), latents).astype(BF16)
+                rows = slice(j * GROUP, (j + 1) * GROUP)
+                lat_out_ref[:, rows, :] = result.reshape(HEADS, GROUP, LATENT)
+            for j, top, total_of in zip(members, tops, totals):
+                stat = jnp.zeros((GROUP, 128), F32)
+                for h in range(HEADS):
+                    part = slice(h * GROUP, (h + 1) * GROUP)
+                    both = jnp.where(at_lane < 3 * HEADS, top[part], total_of[part])
+                    stat = jnp.where(at_lane % HEADS == h, both, stat)
+                hi = stat.astype(BF16).astype(F32)
+                mid = (stat - hi).astype(BF16).astype(F32)
+                low = stat - hi - mid
+                third = (at_lane // HEADS) % 3
+                split = jnp.where(third == 0, hi, jnp.where(third == 1, mid, low))
+                full_ref[j * GROUP : (j + 1) * GROUP, BACK - 128 : BACK] = split.astype(BF16)
         for h in range(HEADS):
             value = dot(lat_out_ref[h], value_ref[:, h * VALUE : (h + 1) * VALUE])
             place = h * VALUE if h < HEADS // 2 else h * VALUE + 128
@@ -237,7 +244,17 @@
     lax.fori_loop(0, (table_ref[1, 0] + PER_CHUNK - 1) // PER_CHUNK, chunk, 0)
 
 
-def index_kernel(idx_ref, weights_ref, keys_ref, out_ref, wide_ref):
+def index_kernel(place_ref, back_ref, idx_ref, weights_ref, keys_ref, out_ref, wide_ref):
+    back = back_ref[...]
+    hi = back.astype(BF16)
+    mid = (back - hi.astype(F32)).astype(BF16)
+    low = (back - hi.astype(F32) - mid.astype(F32)).astype(BF16)
+    lane = iota((TOK, SLOTS), 1)
+    for i in range(PICKS):
+        at = place_ref[:, i : i + 1]
+        pick = ones_where(lane == (at // 8) * CAP + at % 8)
+        far = dot(pick, hi) + dot(pick, mid) + dot(pick, low)
+        out_ref[BLOCKS // 2, :, i * BLOCK : (i + 1) * BLOCK] = far
     stacked = jnp.concatenate(
         [idx_ref[:, g * IDX_DIM : (g + 1) * IDX_DIM] for g in range(IDX_HEADS)], axis=0
     )
@@ -251,7 +268,6 @@
         for g in range(1, IDX_HEADS):
             acc = acc + wide_ref[g] * dots[g * TOK : (g + 1) * TOK]
         out_ref[b // 2] = acc * INDEX_SCALE
-    out_ref[BLOCKS // 2] = jnp.zeros((TOK, 256), F32)
 
 
 def near_kernel(
@@ -288,7 +304,7 @@
     stat_ref[...] = stat
 
 
-def combine_kernel(place_ref, back_ref, near_ref, stat_ref, own_ref, out_ref, index_ref):
+def combine_kernel(place_ref, back_ref, near_ref, stat_ref, out_ref):
     row = iota((TOK, ROWS), 1)
     picks = [row == place_ref[:, i : i + 1] + o for i in range(PICKS) for o in (0, 4)]
     got = dot(jnp.concatenate([ones_where(p) for p in picks], axis=0), back_ref[...])
@@ -298,11 +314,6 @@
         whole = [tail[:, n * HEADS : (n + 1) * HEADS] for n in range(6)]
         far_top.append(whole[0] + whole[1] + whole[2])
         far_sum.append(whole[3] + whole[4] + whole[5])
-        terms = got[(2 * i + 1) * TOK : (2 * i + 2) * TOK, BACK - 128 :]
-        lanes = slice(i * BLOCK, (i + 1) * BLOCK)
-        index_ref[:, lanes] = jnp.where(
-            lax.axis_index("tp") == BLOCKS // 2, terms, own_ref[:, lanes]
-        )
     near_top = stat_ref[:, :HEADS]
     near_sum = stat_ref[:, HEADS : 2 * HEADS]
     top = jnp.maximum(near_top, jnp.maximum(far_top[0], far_top[1]))
@@ -343,7 +354,7 @@
 
 def pack(offsets, blocks, weights, nope, rope, idx):
     out = [shape((ROWS, SEND)), shape((TOK, 128), jnp.int32)]
-    return call(pack_kernel, out, name="pack")(offsets, blocks, weights, nope, rope, idx)
+    return call(pack_kernel, out, name="pack", limit=58)(offsets, blocks, weights, nope, rope, idx)
 
 
 def far_index(sent, keys):
@@ -362,7 +373,7 @@
 ]
 
 
-def far_attention(table, sent, where, index, gathered, lat, rot):
+def far_attention(table, sent, where, gathered, lat, rot):
     scratch = (
         [pltpu.VMEM((16 * SHARDS, 2048), BF16), pltpu.VMEM((SEEN, LATENT), BF16)]
         + WEIGHTS
@@ -381,15 +392,15 @@
         scratch,
         "far_attention",
         8 * 10**9,
-        32,
-        in_specs=[SMEM] + [VMEM] * 4 + [anywhere] * 2,
-    )(table, sent, where, index, rot, gathered, lat)
-
-
-def index_terms(idx, weights, keys):
+        59,
+        in_specs=[SMEM] + [VMEM] * 3 + [anywhere] * 2,
+    )(table, sent, where, rot, gathered, lat)
+
+
+def index_terms(place, back, idx, weights, keys):
     scratch = [pltpu.VMEM((IDX_HEADS, TOK, 256), F32)]
     return call(index_kernel, shape((8, TOK, 256), F32), scratch, "index_terms")(
-        idx, weights, keys
+        place, back, idx, weights, keys
     )
 
 
@@ -400,9 +411,10 @@
     )
 
 
-def combine(place, back, near, stat, own):
-    out = [shape((TOK, HEADS * VALUE)), shape((TOK, 256), F32)]
-    return call(combine_kernel, out, name="combine")(place, back, near, stat, own)
+def combine(place, back, near, stat):
+    return call(combine_kernel, shape((TOK, HEADS * VALUE)), name="combine")(
+        place, back, near, stat
+    )
 
 
 SEQ = ("y", "x", "core")
@@ -435,15 +447,17 @@
     nope = q_nope.reshape(TOK, HEADS * DIM)
     packed, place = pack(owner_offsets.T, local_blocks.T, weights, nope, q_rope, index_queries)
     sent = exchange(packed.reshape(SHARDS, 8, SEND)).reshape(ROWS, SEND)
-    terms = index_terms(index_queries, weights, index_keys)
-    own = lax.psum_scatter(terms, "tp", scatter_dimension=0, tiled=False)
     index, where, table = far_index(sent, index_keys)
-    for bit in (1, 2, 4):
-        index = index + lax.ppermute(index, "tp", [(n, n ^ bit) for n in range(8)])
-    back = far_attention(table, sent, where, index, gathered, cached_latents, rope_keys)
+    index = exchange(index.reshape(SHARDS, CAP, BLOCK)).reshape(SLOTS, BLOCK)
+    terms = index_terms(place, index, index_queries, weights, index_keys)
+    table, terms = lax.optimization_barrier((table, terms))
+    index_scores = lax.psum_scatter(terms, "tp", scatter_dimension=0, tiled=False)
+    back = far_attention(table, sent, where, gathered, cached_latents, rope_keys)
     back = exchange(back.reshape(SHARDS, 8, BACK)).reshape(ROWS, BACK)
     near, stat = near_attention(nope, q_rope, gathered, cached_latents, rope_keys)
-    return combine(place, back, near, stat, own)
+    near, index_scores = lax.optimization_barrier((near, index_scores))
+    attended = combine(place, back, near, stat)
+    return (attended, index_scores)
 
 
 def solution(mesh):

time: 205 us -> 187 us (0.912)
  the two profiles are of different devices: /device:TPU:4 before, /device:TPU:2 now
where the time goes in v2:
time: 187 us; the launch traced here: 186 us
  blocking collectives  84.9 us (45%)
  waiting for transfers between devices  34.5 us (18%)
  Pallas kernels  31.8 us (17%)
  between operations  15.6 us (8%)
  starting transfers between devices  8.86 us (5%)
  local copies, waits for them, and re-layouts  8.66 us (5%)
    all_to_all x2, blocking collectives, exchange(): return lax.all_to_all(value, SEQ, split_axis=0, concat_axis=0, tiled=True)  84.9 us
    reduce_scatter x1, waiting for transfers between devices, on_device(): lax.psum_scatter(terms, 'tp', scatter_dimension=0, tiled=False)  34.2 us
    pallas_call x1, Pallas kernels, far_attention(): call(far_kernel, shape((ROWS, BACK)), scratch, 'far_attention', 8 * 10 **...  12.8 us
    all_to_all x1, starting transfers between devices, exchange(): return lax.all_to_all(value, SEQ, split_axis=0, concat_axis=0, tiled=True)  8.56 us
    pallas_call x1, Pallas kernels, near_attention(): call(near_kernel, out, WEIGHTS, 'near_attention', 8 * 10 ** 9, 32)  8.49 us
    unnamed x34, local copies, waits for them, and re-layouts  7.89 us
    pallas_call x1, Pallas kernels, pack(): call(pack_kernel, out, name='pack', limit=58)  3.86 us
  transfers between devices with their start and end apart: 3, of which 1 were waited for; matrix products, arithmetic and copies ran while one was open for 1% of the time, Pallas kernels for 9%

profile of v2, /device:TPU:2, one launch (start us, length us, event | category | flops | bytes accessed | tf_op | source)
XLA Modules:
  0.0 185.8 jit_solution(10981241098487469384)
XLA Ops:
  8.0 0.0 all-gather.2.cloned.1.call-start
  8.0 0.8 copy.13
  8.8 1.4 pad_maximum_fusion
  10.2 0.0 all-gather.2.cloned.1.call-update
  10.3 1.7 copy.17
  12.0 3.9 %pack.1 = (bf16[512,2176]{1,0:T(8,128)(2,1)}, s32[64,128]{1,0:T(8,128)}) custom-call(s32[2,64]{1,0:T(2,128)} %bitcast.39, s32[2,64]{1,0:T(2,128)} %bitcast.40, bf16[8,64]{1,0:T(8,128)(2,1)} %bitcast.29, bf16[64,2048]{1,0:T(8,128)(2,1)} %bitcast.25, bf16[64,1024]{1,0:T(8,128)(2,1)} %rope_ref.3, bf16[64,1024]{1,0:T(8,128)(2,1)} %idx_ref.3), custom_call_target="tpu_custom_call" | custom-call | flops 1000000000 | bytes 1000000 | tf_op jit(solution)/shard_map/pack/pallas_call | solution.py:357
  15.8 68.8 %all_to_all.15 = bf16[64,8,2176]{2,1,0:T(8,128)(2,1)S(1)} all-to-all(bf16[64,8,2176]{2,1,0:T(8,128)(2,1)} %bitcast.31), channel_id=1, replica_groups=mesh['y'=8,'x'=4,'core'=2,'tp'=8] {'y','x','core'}, dimensions={0} | all-to-all | bytes 4456448 | tf_op jit(solution)/shard_map/all_to_all | solution.py:424
  84.6 0.0 copy-done.4
  84.6 0.0 copy-start.11
  84.6 3.1 %far_index.1 = (f32[256,128]{1,0:T(8,128)S(1)}, bf16[256,512]{1,0:T(8,128)(2,1)S(1)}, s32[8,128]{1,0:T(8,128)S(1)}) custom-call(bf16[512,2176]{1,0:T(8,128)(2,1)S(1)} %bitcast.22, bf16[1792,128]{1,0:T(8,128)(2,1)S(1)} %copy-done.4), custom_call_target="tpu_custom_call" | custom-call | flops 4000000000 | bytes 1000000 | tf_op jit(solution)/shard_map/far_index/pallas_call | solution.py:367
  87.7 0.0 copy-done
  87.8 16.1 %all_to_all.16 = f32[64,4,128]{2,1,0:T(4,128)S(1)} all-to-all(f32[64,4,128]{2,1,0:T(4,128)S(1)} %bitcast.27), channel_id=1, replica_groups=mesh['y'=8,'x'=4,'core'=2,'tp'=8] {'y','x','core'}, dimensions={0} | all-to-all | bytes 262144 | tf_op jit(solution)/shard_map/all_to_all | solution.py:424
  103.9 0.0 copy-done.14
  103.9 1.7 index_terms.1
  105.6 12.8 %far_attention.1 = bf16[512,1152]{1,0:T(8,128)(2,1)} custom-call(s32[8,128]{1,0:T(8,128)} %copy-done.15, bf16[512,2176]{1,0:T(8,128)(2,1)} %bitcast.23, bf16[256,512]{1,0:T(8,128)(2,1)} %copy-done.14, bf16[64,1792]{1,0:T(8,128)(2,1)} %rot_ref.3, bf16[1024,2048]{1,0:T(8,128)(2,1)} %all-gather.2.cloned.1.call-done.all_ref, bf16[1792,512]{1,0:T(8,128)(2,1)} %lat_ref.3), custom_call_target="tpu_custom_call" | custom-call | flops 8000000000 | bytes 1000000 | tf_op jit(solution)/shard_map/far_attention/pallas_call | solution.py:389
  118.4 0.0 copy-start.1
  118.4 0.0 copy-start.3
  118.4 0.0 copy-start.5
  118.4 8.6 %all-to-all-start.2 = ((bf16[64,8,1152]{2,1,0:T(8,128)(2,1)}), bf16[64,8,1152]{2,1,0:T(8,128)(2,1)S(1)}, u32[]{:S(2)}, u32[]{:S(2)}) async-start(bf16[64,8,1152]{2,1,0:T(8,128)(2,1)} %bitcast.32), calls=%async_computation.2 | async-start | bytes 2359296 | tf_op jit(solution)/shard_map/all_to_all | solution.py:424
  127.0 0.3 reduce-scatter.2.cloned.1.call-start
  127.3 0.3 reduce-scatter.2.cloned.1.call-update
  127.6 2.2 %copy-done.2 = bf16[1024,2048]{1,0:T(8,128)(2,1)S(1)} copy-done((bf16[1024,2048]{1,0:T(8,128)(2,1)S(1)}, bf16[1024,2048]{1,0:T(8,128)(2,1)}, u32[]{:S(2)}) %copy-start.2) | copy-done | bytes 4194328
  129.8 0.9 copy-done.7
  130.7 8.5 %near_attention.1 = (bf16[64,2048]{1,0:T(8,128)(2,1)S(1)}, f32[64,128]{1,0:T(8,128)S(1)}) custom-call(bf16[64,2048]{1,0:T(8,128)(2,1)S(1)} %bitcast.26, bf16[64,1024]{1,0:T(8,128)(2,1)S(1)} %copy-done.7, bf16[1024,2048]{1,0:T(8,128)(2,1)S(1)} %copy-done.2, bf16[1792,512]{1,0:T(8,128)(2,1)S(1)} %copy-done.3, bf16[64,1792]{1,0:T(8,128)(2,1)S(1)} %copy-done.5), custom_call_target="tpu_custom_call" | custom-call | flops 8000000000 | bytes 1000000 | tf_op jit(solution)/shard_map/near_attention/pallas_call | solution.py:409
  139.2 0.0 copy-start.9
  139.2 0.7 copy-done.9
  139.9 0.6 copy-done.12
  140.5 34.2 %reduce-scatter.2.cloned.1.call-done = f32[1,64,256]{2,1,0:T(8,128)} async-done(((f32[8,64,256]{2,1,0:T(8,128)}), f32[1,64,256]{2,1,0:T(8,128)}) %reduce-scatter.2.cloned.1.call-update) | async-done | bytes 65552 | tf_op jit(solution)/shard_map/reduce_scatter | solution.py:454
  174.7 0.0 all-to-all-done.2
  174.7 0.9 copy-done.10
  175.7 0.8 copy-done.13
  176.4 1.9 %combine.1 = bf16[64,2048]{1,0:T(8,128)(2,1)} custom-call(s32[64,128]{1,0:T(8,128)S(1)} %copy-done.11, bf16[512,1152]{1,0:T(8,128)(2,1)S(1)} %bitcast.24, bf16[64,2048]{1,0:T(8,128)(2,1)S(1)} %copy-done.10, f32[64,128]{1,0:T(8,128)S(1)} %copy-done.13), custom_call_target="tpu_custom_call" | custom-call | flops 1000000000 | bytes 1000000 | tf_op jit(solution)/shard_map/combine/pallas_call | solution.py:415
  (20 shorter events, 0.0 us)
Async XLA Ops:
  8.0 97.6 %all-gather.2.cloned.1.call-start = ((), (), s32[]{:S(2)}) async-start(), calls=%async_computation.4 | async-start | bytes 4259840 | tf_op jit(solution)/shard_map/all_gather | solution.py:445
  15.8 68.8 %copy-start.4 = (bf16[1792,128]{1,0:T(8,128)(2,1)S(1)}, bf16[1792,128]{1,0:T(8,128)(2,1)}, u32[]{:S(2)}) copy-start(bf16[1792,128]{1,0:T(8,128)(2,1)} %keys_ref.3) | copy-start | bytes 1376260
  84.6 3.2 %copy-start = (bf16[64,8,2176]{2,1,0:T(8,128)(2,1)}, bf16[64,8,2176]{2,1,0:T(8,128)(2,1)S(1)}, u32[]{:S(2)}) copy-start(bf16[64,8,2176]{2,1,0:T(8,128)(2,1)S(1)} %all_to_all.15) | copy-start | bytes 6684676
  84.6 19.3 %copy-start.6 = (bf16[64,1024]{1,0:T(8,128)(2,1)S(1)}, bf16[64,1024]{1,0:T(8,128)(2,1)}, u32[]{:S(2)}) copy-start(bf16[64,1024]{1,0:T(8,128)(2,1)} %idx_ref.3) | copy-start | bytes 393220
  84.6 19.3 %copy-start.8 = (bf16[64,8]{0,1:T(8,128)(2,1)S(1)}, bf16[64,8]{0,1:T(8,128)(2,1)}, u32[]{:S(2)}) copy-start(bf16[64,8]{0,1:T(8,128)(2,1)} %param.14) | copy-start | bytes 3076
  84.6 19.3 %copy-start.11 = (s32[64,128]{1,0:T(8,128)S(1)}, s32[64,128]{1,0:T(8,128)}, u32[]{:S(2)}) copy-start(s32[64,128]{1,0:T(8,128)} %get-tuple-element.13.place_ref) | copy-start | bytes 98308
  87.7 16.2 %copy-start.14 = (bf16[256,512]{1,0:T(8,128)(2,1)}, bf16[256,512]{1,0:T(8,128)(2,1)S(1)}, u32[]{:S(2)}) copy-start(bf16[256,512]{1,0:T(8,128)(2,1)S(1)} %get-tuple-element.18.where_ref) | copy-start | bytes 786436
  87.8 16.2 %copy-start.15 = (s32[8,128]{1,0:T(8,128)}, s32[8,128]{1,0:T(8,128)S(1)}, u32[]{:S(2)}) copy-start(s32[8,128]{1,0:T(8,128)S(1)} %get-tuple-element.17.table_ref) | copy-start | bytes 12292
  118.4 9.2 %copy-start.1 = (bf16[8,8,16,128]{3,1,2,0:T(8,128)(2,1)S(1)}, bf16[8,8,16,128]{3,1,2,0:T(8,128)(2,1)}, u32[]{:S(2)}) copy-start(bf16[8,8,16,128]{3,1,2,0:T(8,128)(2,1)} %copy.17) | copy-start | bytes 786436
  118.4 9.2 %copy-start.3 = (bf16[1792,512]{1,0:T(8,128)(2,1)S(1)}, bf16[1792,512]{1,0:T(8,128)(2,1)}, u32[]{:S(2)}) copy-start(bf16[1792,512]{1,0:T(8,128)(2,1)} %lat_ref.3) | copy-start | bytes 5505028
  118.4 9.2 %copy-start.5 = (bf16[64,1792]{1,0:T(8,128)(2,1)S(1)}, bf16[64,1792]{1,0:T(8,128)(2,1)}, u32[]{:S(2)}) copy-start(bf16[64,1792]{1,0:T(8,128)(2,1)} %rot_ref.3) | copy-start | bytes 688132
  118.4 56.3 %all-to-all-start.2 = ((bf16[64,8,1152]{2,1,0:T(8,128)(2,1)}), bf16[64,8,1152]{2,1,0:T(8,128)(2,1)S(1)}, u32[]{:S(2)}, u32[]{:S(2)}) async-start(bf16[64,8,1152]{2,1,0:T(8,128)(2,1)} %bitcast.32), calls=%async_computation.2 | async-start | bytes 2359296 | tf_op jit(solution)/shard_map/all_to_all | solution.py:424
  127.0 47.8 %reduce-scatter.2.cloned.1.call-start = ((), (), s32[]{:S(2)}) async-start(), calls=%async_computation.5 | async-start | bytes 589824 | tf_op jit(solution)/shard_map/reduce_scatter | solution.py:454
  127.6 2.2 %copy-start.2 = (bf16[1024,2048]{1,0:T(8,128)(2,1)S(1)}, bf16[1024,2048]{1,0:T(8,128)(2,1)}, u32[]{:S(2)}) copy-start(bf16[1024,2048]{1,0:T(8,128)(2,1)} %all-gather.2.cloned.1.call-done.all_ref) | copy-start | bytes 12582916
  129.8 0.9 copy-start.7
  139.2 0.7 copy-start.9
  139.9 0.6 copy-start.12
  174.7 1.0 copy-start.10
  175.7 0.8 copy-start.13
Sparse Core Ops, SparseCore 0:
  12.8 92.5 all-gather.1
Sparse Core Ops, SparseCore 1:
  130.8 43.8 reduce-scatter.1

commit v3 on v2

--- a/solution.py
+++ b/solution.py
@@ -424,6 +424,13 @@
     return lax.all_to_all(value, SEQ, split_axis=0, concat_axis=0, tiled=True)
 
 
+def halves(terms, bit):
+    upper = (lax.axis_index("tp") // bit) % 2
+    sent = lax.dynamic_slice_in_dim(terms, (1 - upper) * bit, bit, 0)
+    kept = lax.dynamic_slice_in_dim(terms, upper * bit, bit, 0)
+    return kept, lax.ppermute(sent, "tp", [(n, n ^ bit) for n in range(8)])
+
+
 def on_device(
     q_nope,
     q_rope,
@@ -451,11 +458,14 @@
     index = exchange(index.reshape(SHARDS, CAP, BLOCK)).reshape(SLOTS, BLOCK)
     terms = index_terms(place, index, index_queries, weights, index_keys)
     table, terms = lax.optimization_barrier((table, terms))
-    index_scores = lax.psum_scatter(terms, "tp", scatter_dimension=0, tiled=False)
+    kept, other = halves(terms, 4)
     back = far_attention(table, sent, where, gathered, cached_latents, rope_keys)
     back = exchange(back.reshape(SHARDS, 8, BACK)).reshape(ROWS, BACK)
     near, stat = near_attention(nope, q_rope, gathered, cached_latents, rope_keys)
-    near, index_scores = lax.optimization_barrier((near, index_scores))
+    near, other = lax.optimization_barrier((near, other))
+    for bit in (2, 1):
+        kept, other = halves(kept + other, bit)
+    index_scores = (kept + other)[0]
     attended = combine(place, back, near, stat)
     return (attended, index_scores)
 

time: 187 us -> 175 us (0.936)
  waiting for transfers between devices: 34.5 us -> 10.7 us
  starting transfers between devices: 8.86 us -> 24.6 us
  local copies, waits for them, and re-layouts: 8.66 us -> 6.29 us
    reduce_scatter x1 -> x0, waiting for transfers between devices: 34.2 us -> none  [on_device(): lax.psum_scatter(terms, 'tp', scatter_dimension=0, tiled=False)]
    ppermute x0 -> x3, starting transfers between devices: none -> 16.2 us  [halves(): return (kept, lax.ppermute(sent, 'tp', [(n, n ^ bit) for n in range(8)]))]
    ppermute x0 -> x3, waiting for transfers between devices: none -> 10.1 us  [halves(): return (kept, lax.ppermute(sent, 'tp', [(n, n ^ bit) for n in range(8)]))]
    unnamed x34 -> x26, local copies, waits for them, and re-layouts: 7.89 us -> 5.46 us
  transfers between devices with their start and end apart: 3 -> 5, of which waited for: 1 -> 3; matrix products, arithmetic and copies ran while one was open for 1% -> 1% of each run, Pallas kernels for 9% -> 9%
where the time goes in v3:
time: 175 us; the launch traced here: 174 us
  blocking collectives  84.8 us (48%)
  Pallas kernels  31 us (18%)
  starting transfers between devices  24.6 us (14%)
  between operations  14.4 us (8%)
  waiting for transfers between devices  10.7 us (6%)
  local copies, waits for them, and re-layouts  6.29 us (4%)
  other arithmetic  2.09 us (1%)
    all_to_all x2, blocking collectives, exchange(): return lax.all_to_all(value, SEQ, split_axis=0, concat_axis=0, tiled=True)  84.8 us
    ppermute x3, starting transfers between devices, halves(): return (kept, lax.ppermute(sent, 'tp', [(n, n ^ bit) for n in range(8)]))  16.2 us
    pallas_call x1, Pallas kernels, far_attention(): call(far_kernel, shape((ROWS, BACK)), scratch, 'far_attention', 8 * 10 **...  12.7 us
    ppermute x3, waiting for transfers between devices, halves(): return (kept, lax.ppermute(sent, 'tp', [(n, n ^ bit) for n in range(8)]))  10.1 us
    pallas_call x1, Pallas kernels, near_attention(): call(near_kernel, out, WEIGHTS, 'near_attention', 8 * 10 ** 9, 32)  8.49 us
    all_to_all x1, starting transfers between devices, exchange(): return lax.all_to_all(value, SEQ, split_axis=0, concat_axis=0, tiled=True)  8.43 us
    unnamed x26, local copies, waits for them, and re-layouts  5.46 us
    pallas_call x1, Pallas kernels, pack(): call(pack_kernel, out, name='pack', limit=58)  3.84 us
  transfers between devices with their start and end apart: 5, of which 3 were waited for; matrix products, arithmetic and copies ran while one was open for 1% of the time, Pallas kernels for 9%

profile of v3, /device:TPU:2, one launch (start us, length us, event | category | flops | bytes accessed | tf_op | source)
XLA Modules:
  0.0 173.9 jit_solution(12998422967666061191)
XLA Ops:
  7.2 0.0 all-gather.2.cloned.1.call-start
  7.2 0.8 copy.13
  8.0 1.4 pad_maximum_fusion
  9.4 0.0 all-gather.2.cloned.1.call-update
  9.4 1.7 copy.17
  11.1 3.8 %pack.1 = (bf16[512,2176]{1,0:T(8,128)(2,1)}, s32[64,128]{1,0:T(8,128)}) custom-call(s32[2,64]{1,0:T(2,128)} %bitcast.39, s32[2,64]{1,0:T(2,128)} %bitcast.40, bf16[8,64]{1,0:T(8,128)(2,1)} %bitcast.30, bf16[64,2048]{1,0:T(8,128)(2,1)} %bitcast.26, bf16[64,1024]{1,0:T(8,128)(2,1)} %rope_ref.3, bf16[64,1024]{1,0:T(8,128)(2,1)} %idx_ref.3), custom_call_target="tpu_custom_call" | custom-call | flops 1000000000 | bytes 1000000 | tf_op jit(solution)/shard_map/pack/pallas_call | solution.py:357
  15.0 68.7 %all_to_all.15 = bf16[64,8,2176]{2,1,0:T(8,128)(2,1)S(1)} all-to-all(bf16[64,8,2176]{2,1,0:T(8,128)(2,1)} %bitcast.32), channel_id=1, replica_groups=mesh['y'=8,'x'=4,'core'=2,'tp'=8] {'y','x','core'}, dimensions={0} | all-to-all | bytes 4456448 | tf_op jit(solution)/shard_map/all_to_all | solution.py:424
  83.7 0.0 copy-start.9
  83.7 3.2 %far_index.1 = (f32[256,128]{1,0:T(8,128)S(1)}, bf16[256,512]{1,0:T(8,128)(2,1)S(1)}, s32[8,128]{1,0:T(8,128)S(1)}) custom-call(bf16[512,2176]{1,0:T(8,128)(2,1)S(1)} %bitcast.23, bf16[1792,128]{1,0:T(8,128)(2,1)S(1)} %copy-done.4), custom_call_target="tpu_custom_call" | custom-call | flops 4000000000 | bytes 1000000 | tf_op jit(solution)/shard_map/far_index/pallas_call | solution.py:367
  86.9 0.0 copy-done
  86.9 0.0 copy-start.10
  86.9 0.0 copy-start.11
  86.9 16.2 %all_to_all.16 = f32[64,4,128]{2,1,0:T(4,128)S(1)} all-to-all(f32[64,4,128]{2,1,0:T(4,128)S(1)} %bitcast.28), channel_id=1, replica_groups=mesh['y'=8,'x'=4,'core'=2,'tp'=8] {'y','x','core'}, dimensions={0} | all-to-all | bytes 262144 | tf_op jit(solution)/shard_map/all_to_all | solution.py:424
  103.1 0.8 index_terms.1
  104.0 0.5 all-gather.2.cloned.1.call-done.all_ref
  104.5 12.7 %far_attention.1 = bf16[512,1152]{1,0:T(8,128)(2,1)} custom-call(s32[8,128]{1,0:T(8,128)} %copy-done.11, bf16[512,2176]{1,0:T(8,128)(2,1)} %bitcast.24, bf16[256,512]{1,0:T(8,128)(2,1)} %copy-done.10, bf16[64,1792]{1,0:T(8,128)(2,1)} %rot_ref.3, bf16[1024,2048]{1,0:T(8,128)(2,1)} %all-gather.2.cloned.1.call-done.all_ref, bf16[1792,512]{1,0:T(8,128)(2,1)} %lat_ref.3), custom_call_target="tpu_custom_call" | custom-call | flops 8000000000 | bytes 1000000 | tf_op jit(solution)/shard_map/far_attention/pallas_call | solution.py:389
  117.2 0.0 copy-start.1
  117.2 0.0 copy-start.5
  117.2 0.0 copy-start.7
  117.3 8.4 %all-to-all-start.2 = ((bf16[64,8,1152]{2,1,0:T(8,128)(2,1)}), bf16[64,8,1152]{2,1,0:T(8,128)(2,1)S(1)}, u32[]{:S(2)}, u32[]{:S(2)}) async-start(bf16[64,8,1152]{2,1,0:T(8,128)(2,1)} %bitcast.33), calls=%async_computation.2 | async-start | bytes 2359296 | tf_op jit(solution)/shard_map/all_to_all | solution.py:424
  125.8 9.3 %collective-permute-start = (f32[4,64,256]{2,1,0:T(8,128)S(1)}, f32[4,64,256]{2,1,0:T(8,128)S(1)}, u32[]{:S(2)}, u32[]{:S(2)}) collective-permute-start(f32[4,64,256]{2,1,0:T(8,128)S(1)} %constant_dynamic-slice_fusion.2), channel_id=1, source_target_pairs={{0,4},{1,5},{2,6},{3,7},{4,0},{5,1},{6,2},{7,3},{8,12},{9,13},{10,... | collective-permute-start | bytes 786440 | tf_op jit(solution)/shard_map/ppermute | solution.py:431
  135.2 2.2 %copy-done.2 = bf16[1024,2048]{1,0:T(8,128)(2,1)S(1)} copy-done((bf16[1024,2048]{1,0:T(8,128)(2,1)S(1)}, bf16[1024,2048]{1,0:T(8,128)(2,1)}, u32[]{:S(2)}) %copy-start.2) | copy-done | bytes 4194328
  137.3 1.5 copy-done.3
  138.8 8.5 %near_attention.1 = (bf16[64,2048]{1,0:T(8,128)(2,1)S(1)}, f32[64,128]{1,0:T(8,128)S(1)}) custom-call(bf16[64,2048]{1,0:T(8,128)(2,1)S(1)} %bitcast.27, bf16[64,1024]{1,0:T(8,128)(2,1)S(1)} %copy-done.7, bf16[1024,2048]{1,0:T(8,128)(2,1)S(1)} %copy-done.2, bf16[1792,512]{1,0:T(8,128)(2,1)S(1)} %copy-done.3, bf16[64,1792]{1,0:T(8,128)(2,1)S(1)} %copy-done.5), custom_call_target="tpu_custom_call" | custom-call | flops 8000000000 | bytes 1000000 | tf_op jit(solution)/shard_map/near_attention/pallas_call | solution.py:409
  147.3 0.0 collective-permute-done
  147.4 4.4 %collective-permute-start.1 = (f32[2,64,256]{2,1,0:T(8,128)S(1)}, f32[2,64,256]{2,1,0:T(8,128)S(1)}, u32[]{:S(2)}, u32[]{:S(2)}) collective-permute-start(f32[2,64,256]{2,1,0:T(8,128)S(1)} %constant_dynamic-slice_fusion.1), channel_id=1, source_target_pairs={{0,2},{1,3},{2,0},{3,1},{4,6},{5,7},{6,4},{7,5},{8,10},{9,11},{10,... | collective-permute-start | bytes 393224 | tf_op jit(solution)/shard_map/ppermute | solution.py:431
  151.9 6.4 %collective-permute-done.1 = f32[2,64,256]{2,1,0:T(8,128)S(1)} collective-permute-done((f32[2,64,256]{2,1,0:T(8,128)S(1)}, f32[2,64,256]{2,1,0:T(8,128)S(1)}, u32[]{:S(2)}, u32[]{:S(2)}) %collective-permute-start.1) | collective-permute-done | bytes 131104 | tf_op jit(solution)/shard_map/ppermute | solution.py:431
  158.3 2.4 %collective-permute-start.2 = (f32[1,64,256]{2,1,0:T(8,128)S(1)}, f32[1,64,256]{2,1,0:T(8,128)S(1)}, u32[]{:S(2)}, u32[]{:S(2)}) collective-permute-start(f32[1,64,256]{2,1,0:T(8,128)S(1)} %constant_dynamic-slice_fusion), channel_id=1, source_target_pairs={{0,1},{1,0},{2,3},{3,2},{4,5},{5,4},{6,7},{7,6},{8,9},{9,8},{10,11... | collective-permute-start | bytes 196616 | tf_op jit(solution)/shard_map/ppermute | solution.py:431
  160.8 3.7 %collective-permute-done.2 = f32[1,64,256]{2,1,0:T(8,128)S(1)} collective-permute-done((f32[1,64,256]{2,1,0:T(8,128)S(1)}, f32[1,64,256]{2,1,0:T(8,128)S(1)}, u32[]{:S(2)}, u32[]{:S(2)}) %collective-permute-start.2) | collective-permute-done | bytes 65568 | tf_op jit(solution)/shard_map/ppermute | solution.py:431
  164.5 0.6 add_bitcast_fusion
  165.1 0.0 all-to-all-done.2
  165.1 1.9 %combine.1 = bf16[64,2048]{1,0:T(8,128)(2,1)} custom-call(s32[64,128]{1,0:T(8,128)S(1)} %copy-done.9, bf16[512,1152]{1,0:T(8,128)(2,1)S(1)} %bitcast.25, bf16[64,2048]{1,0:T(8,128)(2,1)S(1)} %get-tuple-element.21.near_ref, f32[64,128]{1,0:T(8,128)S(1)} %get-tuple-element.22.stat_ref), custom_call_target="tpu_custom_call" | custom-call | flops 1000000000 | bytes 1000000 | tf_op jit(solution)/shard_map/combine/pallas_call | solution.py:415
  (21 shorter events, 0.2 us)
Async XLA Ops:
  7.2 97.3 %all-gather.2.cloned.1.call-start = ((), (), s32[]{:S(2)}) async-start(), calls=%async_computation.3 | async-start | bytes 4259840 | tf_op jit(solution)/shard_map/all_gather | solution.py:452
  15.0 68.7 %copy-start.4 = (bf16[1792,128]{1,0:T(8,128)(2,1)S(1)}, bf16[1792,128]{1,0:T(8,128)(2,1)}, u32[]{:S(2)}) copy-start(bf16[1792,128]{1,0:T(8,128)(2,1)} %keys_ref.3) | copy-start | bytes 1376260
  83.6 3.3 %copy-start = (bf16[64,8,2176]{2,1,0:T(8,128)(2,1)}, bf16[64,8,2176]{2,1,0:T(8,128)(2,1)S(1)}, u32[]{:S(2)}) copy-start(bf16[64,8,2176]{2,1,0:T(8,128)(2,1)S(1)} %all_to_all.15) | copy-start | bytes 6684676
  83.6 19.5 %copy-start.6 = (bf16[64,1024]{1,0:T(8,128)(2,1)S(1)}, bf16[64,1024]{1,0:T(8,128)(2,1)}, u32[]{:S(2)}) copy-start(bf16[64,1024]{1,0:T(8,128)(2,1)} %idx_ref.3) | copy-start | bytes 393220
  83.7 19.5 %copy-start.8 = (bf16[64,8]{0,1:T(8,128)(2,1)S(1)}, bf16[64,8]{0,1:T(8,128)(2,1)}, u32[]{:S(2)}) copy-start(bf16[64,8]{0,1:T(8,128)(2,1)} %param.14) | copy-start | bytes 3076
  83.7 19.5 %copy-start.9 = (s32[64,128]{1,0:T(8,128)S(1)}, s32[64,128]{1,0:T(8,128)}, u32[]{:S(2)}) copy-start(s32[64,128]{1,0:T(8,128)} %get-tuple-element.13.place_ref) | copy-start | bytes 98308
  86.9 17.0 %copy-start.10 = (bf16[256,512]{1,0:T(8,128)(2,1)}, bf16[256,512]{1,0:T(8,128)(2,1)S(1)}, u32[]{:S(2)}) copy-start(bf16[256,512]{1,0:T(8,128)(2,1)S(1)} %get-tuple-element.18.where_ref) | copy-start | bytes 786436
  86.9 17.5 %copy-start.11 = (s32[8,128]{1,0:T(8,128)}, s32[8,128]{1,0:T(8,128)S(1)}, u32[]{:S(2)}) copy-start(s32[8,128]{1,0:T(8,128)S(1)} %get-tuple-element.17.table_ref) | copy-start | bytes 12292
  117.2 17.9 %copy-start.1 = (bf16[8,8,16,128]{3,1,2,0:T(8,128)(2,1)S(1)}, bf16[8,8,16,128]{3,1,2,0:T(8,128)(2,1)}, u32[]{:S(2)}) copy-start(bf16[8,8,16,128]{3,1,2,0:T(8,128)(2,1)} %copy.17) | copy-start | bytes 786436
  117.2 17.9 %copy-start.5 = (bf16[64,1792]{1,0:T(8,128)(2,1)S(1)}, bf16[64,1792]{1,0:T(8,128)(2,1)}, u32[]{:S(2)}) copy-start(bf16[64,1792]{1,0:T(8,128)(2,1)} %rot_ref.3) | copy-start | bytes 688132
  117.2 17.9 %copy-start.7 = (bf16[64,1024]{1,0:T(8,128)(2,1)S(1)}, bf16[64,1024]{1,0:T(8,128)(2,1)}, u32[]{:S(2)}) copy-start(bf16[64,1024]{1,0:T(8,128)(2,1)} %rope_ref.3) | copy-start | bytes 393220
  117.3 47.9 %all-to-all-start.2 = ((bf16[64,8,1152]{2,1,0:T(8,128)(2,1)}), bf16[64,8,1152]{2,1,0:T(8,128)(2,1)S(1)}, u32[]{:S(2)}, u32[]{:S(2)}) async-start(bf16[64,8,1152]{2,1,0:T(8,128)(2,1)} %bitcast.33), calls=%async_computation.2 | async-start | bytes 2359296 | tf_op jit(solution)/shard_map/all_to_all | solution.py:424
  125.8 21.5 %collective-permute-start = (f32[4,64,256]{2,1,0:T(8,128)S(1)}, f32[4,64,256]{2,1,0:T(8,128)S(1)}, u32[]{:S(2)}, u32[]{:S(2)}) collective-permute-start(f32[4,64,256]{2,1,0:T(8,128)S(1)} %constant_dynamic-slice_fusion.2), channel_id=1, source_target_pairs={{0,4},{1,5},{2,6},{3,7},{4,0},{5,1},{6,2},{7,3},{8,12},{9,13},{10,... | collective-permute-start | bytes 786440 | tf_op jit(solution)/shard_map/ppermute | solution.py:431
  135.2 2.2 %copy-start.2 = (bf16[1024,2048]{1,0:T(8,128)(2,1)S(1)}, bf16[1024,2048]{1,0:T(8,128)(2,1)}, u32[]{:S(2)}) copy-start(bf16[1024,2048]{1,0:T(8,128)(2,1)} %all-gather.2.cloned.1.call-done.all_ref) | copy-start | bytes 12582916
  137.3 1.5 copy-start.3
  147.4 10.9 %collective-permute-start.1 = (f32[2,64,256]{2,1,0:T(8,128)S(1)}, f32[2,64,256]{2,1,0:T(8,128)S(1)}, u32[]{:S(2)}, u32[]{:S(2)}) collective-permute-start(f32[2,64,256]{2,1,0:T(8,128)S(1)} %constant_dynamic-slice_fusion.1), channel_id=1, source_target_pairs={{0,2},{1,3},{2,0},{3,1},{4,6},{5,7},{6,4},{7,5},{8,10},{9,11},{10,... | collective-permute-start | bytes 393224 | tf_op jit(solution)/shard_map/ppermute | solution.py:431
  158.3 6.2 %collective-permute-start.2 = (f32[1,64,256]{2,1,0:T(8,128)S(1)}, f32[1,64,256]{2,1,0:T(8,128)S(1)}, u32[]{:S(2)}, u32[]{:S(2)}) collective-permute-start(f32[1,64,256]{2,1,0:T(8,128)S(1)} %constant_dynamic-slice_fusion), channel_id=1, source_target_pairs={{0,1},{1,0},{2,3},{3,2},{4,5},{5,4},{6,7},{7,6},{8,9},{9,8},{10,11... | collective-permute-start | bytes 196616 | tf_op jit(solution)/shard_map/ppermute | solution.py:431
Sparse Core Ops, SparseCore 0:
  11.9 92.4 all-gather.1
